TPU v7x, 512 devices: a whole 4x4x16 slice. The times are simulated.
512 devices in a mesh: grp: 8 (over z_hi, core), pair: 64 (over y, x, z_lo).
Axes of the slice: x: 4, y: 4, z: 16 (z_hi: 4, z_lo: 4; z = z_hi * 4 + z_lo), core: 2. Of those that a mesh axis runs over, the one named last changes fastest.
Arguments:
- embeddings: bfloat16 [786432, 768], P(('grp', 'pair')), parts along dimension 0
- cluster_ids: int32 [786432], P(('grp', 'pair')), parts along dimension 0, may hold values from 0 to 3, as said below
- row_counts: int32 [512], P(('grp', 'pair')), parts along dimension 0, may hold values from 1 to 1536, 73728 in all
Outputs:
- best_cosine: float32 [786432], P(('grp', 'pair')), parts along dimension 0
There are 8 independent parts, one for each index of `grp`. A program takes and returns all parts, laid end to end along the dimension named above; each array names one. Nothing has to cross between parts.
Inputs may be any that keep to these rules, and one draw needn't show every extreme that they name: `cluster_ids`: every cluster number occurs.
All inputs are finite; a program needn't handle non-finite values. No bound on the sum of `row_counts` on one device may be relied on, other than what follows from the above.
Results may differ from a plain program's by a relative error of at most 0.00037.
Values may be sent and summed in bfloat16 or wider, within the bound.
No kernel may reach another device: no remote copies, remote signals or barrier semaphores. Data moves between devices by JAX's collectives and lax.ppermute only.
A program may use at most 64 MiB of HBM per device.

v0:
```python
import jax
import jax.numpy as jnp
from jax import lax
from jax.sharding import PartitionSpec as P

ROUNDS = 4


def swapped(block, axis, bit):
    count = lax.axis_size(axis)
    route = []
    for low in range(count):
        high = low | 1 << bit
        if high != low and high < count:
            route += [(low, high), (high, low)]
    return lax.ppermute(block, axis, route)


def masked_max(left, left_tag, right, right_tag):
    tile = lax.dot_general(
        left, right, (((1,), (1,)), ((), ())), preferred_element_type=jnp.float32
    )
    same = (left_tag[:, None] == right_tag[None, :]) & (left_tag[:, None] >= 0.0)
    tile = jnp.where(same, tile, -1.0)
    return (jnp.max(tile, axis=1), jnp.max(tile, axis=0))


def swap_blocks(normed, tagged, bit):
    return swapped((normed, tagged), "pair", bit)


def swap_partials(values, bit):
    return swapped(values, "pair", bit)


def per_device(embeddings, cluster_ids, row_counts):
    rows = embeddings.shape[0]
    half = rows // 2
    wide = embeddings.astype(jnp.float32)
    squared = jnp.sum(wide * wide, axis=1, keepdims=True)
    normed = (wide * lax.rsqrt(squared + 1e-06)).astype(jnp.bfloat16)
    valid = jnp.arange(rows, dtype=jnp.int32) < row_counts[0]
    tagged = jnp.where(valid, cluster_ids, -1).astype(jnp.bfloat16)
    levels = lax.axis_size("pair").bit_length() - 1
    bits = [levels - 1 - step for step in range(ROUNDS)]
    filler = jnp.full((half,), -1.0, jnp.float32)
    best = jnp.full((rows,), -1.0, jnp.float32)
    for bit in bits:
        part, part_tag = swap_blocks(normed, tagged, bit)
        upper = jnp.bitwise_and(jnp.right_shift(lax.axis_index("pair"), bit), 1)

        def lower_side(unused):
            row_best, col_best = masked_max(normed[:half], tagged[:half], part, part_tag)
            return (jnp.concatenate([row_best, filler]), col_best)

        def upper_side(unused):
            row_best, col_best = masked_max(normed, tagged, part[half:], part_tag[half:])
            return (row_best, jnp.concatenate([col_best, filler]))

        keep, outgoing = lax.cond(upper == 1, upper_side, lower_side, 0)
        incoming = swap_partials(outgoing, bit)
        joined = jnp.concatenate([keep[:half], incoming[:half]])
        found = jnp.where(upper == 1, jnp.maximum(keep, incoming), joined)
        best = jnp.maximum(best, found)
    return best


def solution(mesh):
    return jax.shard_map(
        per_device,
        mesh=mesh,
        in_specs=(P(("grp", "pair"), None), P(("grp", "pair")), P(("grp", "pair"))),
        out_specs=P(("grp", "pair")),
        check_vma=False,
    )
```

profile of v0, /device:TPU:6, one launch (start us, length us, event | category | flops | bytes accessed | tf_op | source)
XLA Modules:
  0.0 158.1 jit_solution(17666249456501600782)
XLA Ops:
  0.0 2.3 %fusion.32 = f32[1536]{0:T(1024)S(1)} fusion(bf16[1536,768]{1,0:T(8,128)(2,1)} %param.11), kind=kLoop, calls=%fused_computation.50 | loop fusion | flops 3537408 | bytes 2365440 | tf_op jit(solution)/shard_map/reduce_sum | solution.py:40
  2.4 0.0 copy-done
  2.4 0.4 fusion.33
  2.8 2.7 %collective-permute-start.10 = (bf16[1536,768]{1,0:T(8,128)(2,1)S(1)}, bf16[1536,768]{1,0:T(8,128)(2,1)S(1)}, u32[]{:S(2)}, u32[]{:S(2)}) collective-permute-start(bf16[1536,768]{1,0:T(8,128)(2,1)S(1)} %fusion.33), channel_id=1, source_target_pairs={{0,4},{4,0},{1,5},{5,1},{2,6},{6,2},{3,7},{7,3},{8,12},{12,8},{9,1... | collective-permute-start | bytes 7077896 | tf_op jit(solution)/shard_map/ppermute | solution.py:16
  5.6 8.4 %collective-permute-start.7 = (bf16[1536,768]{1,0:T(8,128)(2,1)S(1)}, bf16[1536,768]{1,0:T(8,128)(2,1)}, u32[]{:S(2)}, u32[]{:S(2)}) collective-permute-start(bf16[1536,768]{1,0:T(8,128)(2,1)S(1)} %fusion.33), channel_id=1, source_target_pairs={{0,8},{8,0},{1,9},{9,1},{2,10},{10,2},{3,11},{11,3},{4,12},{12,4},... | collective-permute-start | bytes 7077896 | tf_op jit(solution)/shard_map/ppermute | solution.py:16
  14.0 1.9 %collective-permute-start.4 = (bf16[1536,768]{1,0:T(8,128)(2,1)S(1)}, bf16[1536,768]{1,0:T(8,128)(2,1)}, u32[]{:S(2)}, u32[]{:S(2)}) collective-permute-start(bf16[1536,768]{1,0:T(8,128)(2,1)S(1)} %fusion.33), channel_id=1, source_target_pairs={{0,16},{16,0},{1,17},{17,1},{2,18},{18,2},{3,19},{19,3},{4,20},{20... | collective-permute-start | bytes 7077896 | tf_op jit(solution)/shard_map/ppermute | solution.py:16
  15.9 1.9 %collective-permute-start.1 = (bf16[1536,768]{1,0:T(8,128)(2,1)S(1)}, bf16[1536,768]{1,0:T(8,128)(2,1)}, u32[]{:S(2)}, u32[]{:S(2)}) collective-permute-start(bf16[1536,768]{1,0:T(8,128)(2,1)S(1)} %fusion.33), channel_id=1, source_target_pairs={{0,32},{32,0},{1,33},{33,1},{2,34},{34,2},{3,35},{35,3},{4,36},{36... | collective-permute-start | bytes 7077896 | tf_op jit(solution)/shard_map/ppermute | solution.py:16
  18.5 1.9 %collective-permute-start.9 = (bf16[1536]{0:T(1024)(128)(2,1)S(1)}, bf16[1536]{0:T(1024)(128)(2,1)S(1)}, u32[]{:S(2)}, u32[]{:S(2)}) collective-permute-start(bf16[1536]{0:T(1024)(128)(2,1)S(1)} %select_convert_fusion), channel_id=1, source_target_pairs={{0,4},{4,0},{1,5},{5,1},{2,6},{6,2},{3,7},{7,3},{8,12},{12,8},{9,1... | collective-permute-start | bytes 9224 | tf_op jit(solution)/shard_map/ppermute | solution.py:16
  20.4 87.9 %collective-permute-done.9 = bf16[1536]{0:T(1024)(128)(2,1)S(1)} collective-permute-done((bf16[1536]{0:T(1024)(128)(2,1)S(1)}, bf16[1536]{0:T(1024)(128)(2,1)S(1)}, u32[]{:S(2)}, u32[]{:S(2)}) %collective-permute-start.9) | collective-permute-done | bytes 3104 | tf_op jit(solution)/shard_map/ppermute | solution.py:16
  108.4 3.3 %collective-permute-start.6 = (bf16[1536]{0:T(1024)(128)(2,1)S(1)}, bf16[1536]{0:T(1024)(128)(2,1)S(1)}, u32[]{:S(2)}, u32[]{:S(2)}) collective-permute-start(bf16[1536]{0:T(1024)(128)(2,1)S(1)} %select_convert_fusion), channel_id=1, source_target_pairs={{0,8},{8,0},{1,9},{9,1},{2,10},{10,2},{3,11},{11,3},{4,12},{12,4},... | collective-permute-start | bytes 9224 | tf_op jit(solution)/shard_map/ppermute | solution.py:16
  111.7 3.7 %collective-permute-done.6 = bf16[1536]{0:T(1024)(128)(2,1)S(1)} collective-permute-done((bf16[1536]{0:T(1024)(128)(2,1)S(1)}, bf16[1536]{0:T(1024)(128)(2,1)S(1)}, u32[]{:S(2)}, u32[]{:S(2)}) %collective-permute-start.6) | collective-permute-done | bytes 3104 | tf_op jit(solution)/shard_map/ppermute | solution.py:16
  115.4 3.5 %collective-permute-start.3 = (bf16[1536]{0:T(1024)(128)(2,1)S(1)}, bf16[1536]{0:T(1024)(128)(2,1)S(1)}, u32[]{:S(2)}, u32[]{:S(2)}) collective-permute-start(bf16[1536]{0:T(1024)(128)(2,1)S(1)} %select_convert_fusion), channel_id=1, source_target_pairs={{0,16},{16,0},{1,17},{17,1},{2,18},{18,2},{3,19},{19,3},{4,20},{20... | collective-permute-start | bytes 9224 | tf_op jit(solution)/shard_map/ppermute | solution.py:16
  118.9 1.5 copy-done.2
  120.3 4.8 %collective-permute-start = (bf16[1536]{0:T(1024)(128)(2,1)S(1)}, bf16[1536]{0:T(1024)(128)(2,1)S(1)}, u32[]{:S(2)}, u32[]{:S(2)}) collective-permute-start(bf16[1536]{0:T(1024)(128)(2,1)S(1)} %select_convert_fusion), channel_id=1, source_target_pairs={{0,32},{32,0},{1,33},{33,1},{2,34},{34,2},{3,35},{35,3},{4,36},{36... | collective-permute-start | bytes 9224 | tf_op jit(solution)/shard_map/ppermute | solution.py:16
  125.1 4.3 %conditional.7 = (f32[1536]{0:T(1024)S(1)}, f32[1536]{0:T(1024)S(1)}) conditional(s32[]{:T(128)} %convert_element_type.27, (bf16[1536]{0:T(1024)(128)(2,1)S(1)}, bf16[1536]{0:T(1024)(128)(2,1)S(1)}, bf16[1536,768]{1,0:T(8,128)(2,1)S(1)}, bf16[1536,768]{1,0:T(8,128)(2,1)}) %tuple.61, (bf16[1536]{0:T(1024)(128)(2,1)S(1)}, ...), branch_computations={%region_19.22_spmd, %region_22.25_spmd} | conditional | flops 1820196096 | bytes 3571220 | solution.py:60
  125.2 4.2 %fusion.28 = (f32[768]{0:T(1024)S(1)}, f32[1536]{0:T(1024)S(1)}) fusion(pred[1536]{0:T(1024)(128)(4,1)S(1)} %broadcast_compare_fusion.7, bf16[768]{0:T(1024)(128)(2,1)S(1)} %slice.62, bf16[1536]{0:T(1024)(128)(2,1)S(1)} %get-tuple-element.97, bf16[1536,768]{1,0:T(8,128)(2,1)S(1)} %get-tuple-element.99, bf16[1536,768]{1,0:T(8,128)(2,1)} %get-tuple-element.100), kind=kOutput, calls=%fused_computation.43 | convolution fusion | flops 1820194560 | bytes 3554304 | tf_op jit(solution)/shard_map/cond/branch_1_fun/dot_general | solution.py:20
  129.4 2.8 %collective-permute-start.11 = (f32[1536]{0:T(1024)S(1)}, f32[1536]{0:T(1024)S(1)}, u32[]{:S(2)}, u32[]{:S(2)}) collective-permute-start(f32[1536]{0:T(1024)S(1)} %get-tuple-element.116), channel_id=1, source_target_pairs={{0,4},{4,0},{1,5},{5,1},{2,6},{6,2},{3,7},{7,3},{8,12},{12,8},{9,1... | collective-permute-start | bytes 18440 | tf_op jit(solution)/shard_map/ppermute | solution.py:16
  132.3 4.3 %conditional.6 = (f32[1536]{0:T(1024)S(1)}, f32[1536]{0:T(1024)S(1)}) conditional(s32[]{:T(128)} %convert_element_type.26, (bf16[1536]{0:T(1024)(128)(2,1)S(1)}, bf16[1536]{0:T(1024)(128)(2,1)S(1)}, bf16[1536,768]{1,0:T(8,128)(2,1)S(1)}, bf16[1536,768]{1,0:T(8,128)(2,1)}) %tuple.41, (bf16[1536]{0:T(1024)(128)(2,1)S(1)}, ...), branch_computations={%region_13.16_spmd, %region_16.19_spmd} | conditional | flops 1820196096 | bytes 3571220 | solution.py:60
  132.3 4.2 %fusion.20 = (f32[768]{0:T(1024)S(1)}, f32[1536]{0:T(1024)S(1)}) fusion(pred[1536]{0:T(1024)(128)(4,1)S(1)} %broadcast_compare_fusion.5, bf16[768]{0:T(1024)(128)(2,1)S(1)} %slice.58, bf16[1536]{0:T(1024)(128)(2,1)S(1)} %get-tuple-element.89, bf16[1536,768]{1,0:T(8,128)(2,1)S(1)} %get-tuple-element.91, bf16[1536,768]{1,0:T(8,128)(2,1)} %get-tuple-element.92), kind=kOutput, calls=%fused_computation.31 | convolution fusion | flops 1820194560 | bytes 3554304 | tf_op jit(solution)/shard_map/cond/branch_1_fun/dot_general | solution.py:20
  136.5 0.0 collective-permute-done.3
  136.6 3.1 %collective-permute-start.8 = (f32[1536]{0:T(1024)S(1)}, f32[1536]{0:T(1024)S(1)}, u32[]{:S(2)}, u32[]{:S(2)}) collective-permute-start(f32[1536]{0:T(1024)S(1)} %get-tuple-element.114), channel_id=1, source_target_pairs={{0,8},{8,0},{1,9},{9,1},{2,10},{10,2},{3,11},{11,3},{4,12},{12,4},... | collective-permute-start | bytes 18440 | tf_op jit(solution)/shard_map/ppermute | solution.py:16
  139.6 0.0 collective-permute-done.4
  139.7 4.4 %conditional.5 = (f32[1536]{0:T(1024)S(1)}, f32[1536]{0:T(1024)S(1)}) conditional(s32[]{:T(128)} %convert_element_type.25, (bf16[1536]{0:T(1024)(128)(2,1)S(1)}, bf16[1536]{0:T(1024)(128)(2,1)S(1)}, bf16[1536,768]{1,0:T(8,128)(2,1)S(1)}, bf16[1536,768]{1,0:T(8,128)(2,1)}) %tuple.39, (bf16[1536]{0:T(1024)(128)(2,1)S(1)}, ...), branch_computations={%region_7.10_spmd, %region_10.13_spmd} | conditional | flops 1820196096 | bytes 3571220 | solution.py:60
  139.7 4.3 %fusion.8 = (f32[1536]{0:T(1024)S(1)}, f32[768]{0:T(1024)S(1)}) fusion(pred[768]{0:T(1024)(128)(4,1)S(1)} %broadcast_compare_fusion.2, bf16[1536]{0:T(1024)(128)(2,1)S(1)} %get-tuple-element.78, bf16[768]{0:T(1024)(128)(2,1)S(1)} %slice.52, bf16[1536,768]{1,0:T(8,128)(2,1)} %get-tuple-element.80, bf16[1536,768]{1,0:T(8,128)(2,1)S(1)} %get-tuple-element.79), kind=kOutput, calls=%fused_computation.13 | convolution fusion | flops 1820194560 | bytes 3555328 | tf_op jit(solution)/shard_map/cond/branch_0_fun/dot_general | solution.py:20
  144.0 2.0 %collective-permute-start.5 = (f32[1536]{0:T(1024)S(1)}, f32[1536]{0:T(1024)S(1)}, u32[]{:S(2)}, u32[]{:S(2)}) collective-permute-start(f32[1536]{0:T(1024)S(1)} %get-tuple-element.112), channel_id=1, source_target_pairs={{0,16},{16,0},{1,17},{17,1},{2,18},{18,2},{3,19},{19,3},{4,20},{20... | collective-permute-start | bytes 18440 | tf_op jit(solution)/shard_map/ppermute | solution.py:16
  146.0 0.0 collective-permute-done.1
  146.0 4.4 %conditional.4 = (f32[1536]{0:T(1024)S(1)}, f32[1536]{0:T(1024)S(1)}) conditional(s32[]{:T(128)} %convert_element_type.21, (bf16[1536]{0:T(1024)(128)(2,1)S(1)}, bf16[1536]{0:T(1024)(128)(2,1)S(1)}, bf16[1536,768]{1,0:T(8,128)(2,1)S(1)}, bf16[1536,768]{1,0:T(8,128)(2,1)}) %tuple.37, (bf16[1536]{0:T(1024)(128)(2,1)S(1)}, ...), branch_computations={%region_1.4_spmd, %region_4.7_spmd} | conditional | flops 1820196096 | bytes 3571220 | solution.py:60
  146.1 4.3 %fusion = (f32[1536]{0:T(1024)S(1)}, f32[768]{0:T(1024)S(1)}) fusion(pred[768]{0:T(1024)(128)(4,1)S(1)} %broadcast_compare_fusion, bf16[1536]{0:T(1024)(128)(2,1)S(1)} %get-tuple-element.70, bf16[768]{0:T(1024)(128)(2,1)S(1)} %slice.48, bf16[1536,768]{1,0:T(8,128)(2,1)} %get-tuple-element.72, bf16[1536,768]{1,0:T(8,128)(2,1)S(1)} %get-tuple-element.71), kind=kOutput, calls=%fused_computation.1 | convolution fusion | flops 1820194560 | bytes 3555328 | tf_op jit(solution)/shard_map/cond/branch_0_fun/dot_general | solution.py:20
  150.4 3.1 %collective-permute-start.2 = (f32[1536]{0:T(1024)S(1)}, f32[1536]{0:T(1024)S(1)}, u32[]{:S(2)}, u32[]{:S(2)}) collective-permute-start(f32[1536]{0:T(1024)S(1)} %get-tuple-element.110), channel_id=1, source_target_pairs={{0,32},{32,0},{1,33},{33,1},{2,34},{34,2},{3,35},{35,3},{4,36},{36... | collective-permute-start | bytes 18440 | tf_op jit(solution)/shard_map/ppermute | solution.py:16
  153.6 0.0 collective-permute-done.8
  153.6 3.8 %collective-permute-done.2 = f32[1536]{0:T(1024)S(1)} collective-permute-done((f32[1536]{0:T(1024)S(1)}, f32[1536]{0:T(1024)S(1)}, u32[]{:S(2)}, u32[]{:S(2)}) %collective-permute-start.2) | collective-permute-done | bytes 6176 | tf_op jit(solution)/shard_map/ppermute | solution.py:16
  157.4 0.6 fusion.37
  (31 shorter events, 0.1 us)
Async XLA Ops:
  0.0 2.4 %copy-start = (bf16[1536,768]{1,0:T(8,128)(2,1)S(1)}, bf16[1536,768]{1,0:T(8,128)(2,1)}, u32[]{:S(2)}) copy-start(bf16[1536,768]{1,0:T(8,128)(2,1)} %param.11) | copy-start | bytes 7077892
  2.4 16.1 %copy-start.1 = (s32[1536]{0:T(1024)S(1)}, s32[1536]{0:T(1024)}, u32[]{:S(2)}) copy-start(s32[1536]{0:T(1024)} %param.12) | copy-start | bytes 18436
  2.8 116.0 %collective-permute-start.10 = (bf16[1536,768]{1,0:T(8,128)(2,1)S(1)}, bf16[1536,768]{1,0:T(8,128)(2,1)S(1)}, u32[]{:S(2)}, u32[]{:S(2)}) collective-permute-start(bf16[1536,768]{1,0:T(8,128)(2,1)S(1)} %fusion.33), channel_id=1, source_target_pairs={{0,4},{4,0},{1,5},{5,1},{2,6},{6,2},{3,7},{7,3},{8,12},{12,8},{9,1... | collective-permute-start | bytes 7077896 | tf_op jit(solution)/shard_map/ppermute | solution.py:16
  5.6 123.8 %collective-permute-start.7 = (bf16[1536,768]{1,0:T(8,128)(2,1)S(1)}, bf16[1536,768]{1,0:T(8,128)(2,1)}, u32[]{:S(2)}, u32[]{:S(2)}) collective-permute-start(bf16[1536,768]{1,0:T(8,128)(2,1)S(1)} %fusion.33), channel_id=1, source_target_pairs={{0,8},{8,0},{1,9},{9,1},{2,10},{10,2},{3,11},{11,3},{4,12},{12,4},... | collective-permute-start | bytes 7077896 | tf_op jit(solution)/shard_map/ppermute | solution.py:16
  14.0 125.7 %collective-permute-start.4 = (bf16[1536,768]{1,0:T(8,128)(2,1)S(1)}, bf16[1536,768]{1,0:T(8,128)(2,1)}, u32[]{:S(2)}, u32[]{:S(2)}) collective-permute-start(bf16[1536,768]{1,0:T(8,128)(2,1)S(1)} %fusion.33), channel_id=1, source_target_pairs={{0,16},{16,0},{1,17},{17,1},{2,18},{18,2},{3,19},{19,3},{4,20},{20... | collective-permute-start | bytes 7077896 | tf_op jit(solution)/shard_map/ppermute | solution.py:16
  15.9 130.1 %collective-permute-start.1 = (bf16[1536,768]{1,0:T(8,128)(2,1)S(1)}, bf16[1536,768]{1,0:T(8,128)(2,1)}, u32[]{:S(2)}, u32[]{:S(2)}) collective-permute-start(bf16[1536,768]{1,0:T(8,128)(2,1)S(1)} %fusion.33), channel_id=1, source_target_pairs={{0,32},{32,0},{1,33},{33,1},{2,34},{34,2},{3,35},{35,3},{4,36},{36... | collective-permute-start | bytes 7077896 | tf_op jit(solution)/shard_map/ppermute | solution.py:16
  18.5 89.9 %collective-permute-start.9 = (bf16[1536]{0:T(1024)(128)(2,1)S(1)}, bf16[1536]{0:T(1024)(128)(2,1)S(1)}, u32[]{:S(2)}, u32[]{:S(2)}) collective-permute-start(bf16[1536]{0:T(1024)(128)(2,1)S(1)} %select_convert_fusion), channel_id=1, source_target_pairs={{0,4},{4,0},{1,5},{5,1},{2,6},{6,2},{3,7},{7,3},{8,12},{12,8},{9,1... | collective-permute-start | bytes 9224 | tf_op jit(solution)/shard_map/ppermute | solution.py:16
  108.4 7.0 %collective-permute-start.6 = (bf16[1536]{0:T(1024)(128)(2,1)S(1)}, bf16[1536]{0:T(1024)(128)(2,1)S(1)}, u32[]{:S(2)}, u32[]{:S(2)}) collective-permute-start(bf16[1536]{0:T(1024)(128)(2,1)S(1)} %select_convert_fusion), channel_id=1, source_target_pairs={{0,8},{8,0},{1,9},{9,1},{2,10},{10,2},{3,11},{11,3},{4,12},{12,4},... | collective-permute-start | bytes 9224 | tf_op jit(solution)/shard_map/ppermute | solution.py:16
  115.4 21.2 %collective-permute-start.3 = (bf16[1536]{0:T(1024)(128)(2,1)S(1)}, bf16[1536]{0:T(1024)(128)(2,1)S(1)}, u32[]{:S(2)}, u32[]{:S(2)}) collective-permute-start(bf16[1536]{0:T(1024)(128)(2,1)S(1)} %select_convert_fusion), channel_id=1, source_target_pairs={{0,16},{16,0},{1,17},{17,1},{2,18},{18,2},{3,19},{19,3},{4,20},{20... | collective-permute-start | bytes 9224 | tf_op jit(solution)/shard_map/ppermute | solution.py:16
  118.9 1.5 copy-start.2
  120.3 25.7 %collective-permute-start = (bf16[1536]{0:T(1024)(128)(2,1)S(1)}, bf16[1536]{0:T(1024)(128)(2,1)S(1)}, u32[]{:S(2)}, u32[]{:S(2)}) collective-permute-start(bf16[1536]{0:T(1024)(128)(2,1)S(1)} %select_convert_fusion), channel_id=1, source_target_pairs={{0,32},{32,0},{1,33},{33,1},{2,34},{34,2},{3,35},{35,3},{4,36},{36... | collective-permute-start | bytes 9224 | tf_op jit(solution)/shard_map/ppermute | solution.py:16
  129.4 24.1 %collective-permute-start.11 = (f32[1536]{0:T(1024)S(1)}, f32[1536]{0:T(1024)S(1)}, u32[]{:S(2)}, u32[]{:S(2)}) collective-permute-start(f32[1536]{0:T(1024)S(1)} %get-tuple-element.116), channel_id=1, source_target_pairs={{0,4},{4,0},{1,5},{5,1},{2,6},{6,2},{3,7},{7,3},{8,12},{12,8},{9,1... | collective-permute-start | bytes 18440 | tf_op jit(solution)/shard_map/ppermute | solution.py:16
  136.6 17.0 %collective-permute-start.8 = (f32[1536]{0:T(1024)S(1)}, f32[1536]{0:T(1024)S(1)}, u32[]{:S(2)}, u32[]{:S(2)}) collective-permute-start(f32[1536]{0:T(1024)S(1)} %get-tuple-element.114), channel_id=1, source_target_pairs={{0,8},{8,0},{1,9},{9,1},{2,10},{10,2},{3,11},{11,3},{4,12},{12,4},... | collective-permute-start | bytes 18440 | tf_op jit(solution)/shard_map/ppermute | solution.py:16
  144.0 9.6 %collective-permute-start.5 = (f32[1536]{0:T(1024)S(1)}, f32[1536]{0:T(1024)S(1)}, u32[]{:S(2)}, u32[]{:S(2)}) collective-permute-start(f32[1536]{0:T(1024)S(1)} %get-tuple-element.112), channel_id=1, source_target_pairs={{0,16},{16,0},{1,17},{17,1},{2,18},{18,2},{3,19},{19,3},{4,20},{20... | collective-permute-start | bytes 18440 | tf_op jit(solution)/shard_map/ppermute | solution.py:16
  150.4 7.0 %collective-permute-start.2 = (f32[1536]{0:T(1024)S(1)}, f32[1536]{0:T(1024)S(1)}, u32[]{:S(2)}, u32[]{:S(2)}) collective-permute-start(f32[1536]{0:T(1024)S(1)} %get-tuple-element.110), channel_id=1, source_target_pairs={{0,32},{32,0},{1,33},{33,1},{2,34},{34,2},{3,35},{35,3},{4,36},{36... | collective-permute-start | bytes 18440 | tf_op jit(solution)/shard_map/ppermute | solution.py:16
where the time goes:
time: 161 us; the launch traced here: 158 us
  waiting for transfers between devices  95.4 us (59%)
  starting transfers between devices  39.5 us (25%)
  matrix products  17 us (11%)
  other arithmetic  3.44 us (2%)
    ppermute x12, waiting for transfers between devices, swapped(): return lax.ppermute(block, axis, route)  95.4 us
    ppermute x12, starting transfers between devices, swapped(): return lax.ppermute(block, axis, route)  39.5 us
    dot_general x4, matrix products, masked_max(): lax.dot_general(left, right, (((1,), (1,)), ((), ())), preferred_element_...  17 us
  transfers between devices with their start and end apart: 12, of which 3 were waited for; matrix products, arithmetic and copies ran while one was open for 11% of the time, Pallas kernels for 0%

commit v1 on v0

v1 whole, which is shorter than its diff:
```python
import functools

import jax
import jax.numpy as jnp
from jax import lax
from jax.experimental import pallas as pl
from jax.experimental.pallas import tpu as pltpu
from jax.sharding import PartitionSpec as P

LANES = 128
TAG_ROWS = 16
CHUNKS = (512, 768, 256)
AXES = ("grp", "pair")


def routes(grp, pair):
    side = 4
    rest = pair // (side * side)
    near, far = [], []
    for g in range(grp):
        for y in range(side):
            for x in range(side):
                for z in range(rest):

                    def at(v, u):
                        return g * pair + (v * side + u) * rest + z

                    owns_y = (y in (1, 2)) ^ (x in (1, 2)) ^ (g % 2 == 1)
                    here = at(y, x)
                    near.append((here, at(y, x ^ 1) if owns_y else at(y ^ 1, x)))
                    far.append((here, at(3 - y, x) if owns_y else at(y, 3 - x)))
    return near, far


def normalize(tagged, first, count):
    def kernel(*refs):
        if tagged:
            count_ref, ids_ref, rows_ref, out_ref = refs
        else:
            rows_ref, out_ref = refs
        wide = rows_ref[...].astype(jnp.float32)
        squared = jnp.sum(wide * wide, axis=1, keepdims=True)
        out_ref[0:count, :] = (wide * lax.rsqrt(squared + 1e-06)).astype(jnp.bfloat16)
        if tagged:
            ids = ids_ref[...]
            place = lax.broadcasted_iota(jnp.int32, ids.shape, 0) * LANES
            place = place + lax.broadcasted_iota(jnp.int32, ids.shape, 1)
            tags = jnp.where(place < count_ref[0], ids, -1).astype(jnp.float32)
            spare = jnp.full((TAG_ROWS - ids.shape[0], LANES), -1.0, jnp.float32)
            tags = jnp.concatenate([tags, spare], axis=0).astype(jnp.bfloat16)
            out_ref[count:, 0:LANES] = tags
            out_ref[count:, LANES:] = jnp.zeros((TAG_ROWS, out_ref.shape[1] - LANES), jnp.bfloat16)

    def call(rows, *extra):
        width = rows.shape[1]
        step = count if tagged else 256
        total = count + (TAG_ROWS if tagged else 0)
        specs = [pl.BlockSpec((step, width), lambda i: (i + first // step, 0))]
        if tagged:
            specs = [
                pl.BlockSpec(memory_space=pltpu.SMEM),
                pl.BlockSpec(extra[1].shape, lambda i: (0, 0)),
            ] + specs
        return pl.pallas_call(
            kernel if tagged else kernel_of_step(step),
            grid=(count // step,),
            in_specs=specs,
            out_specs=pl.BlockSpec((total if tagged else step, width), lambda i: (i, 0)),
            out_shape=jax.ShapeDtypeStruct((total, width), jnp.bfloat16),
            cost_estimate=pl.CostEstimate(flops=4 * count * width, bytes_accessed=4 * count * width, transcendentals=count),
            name="normalize",
        )(*extra, rows)

    def kernel_of_step(step):
        def body(rows_ref, out_ref):
            wide = rows_ref[...].astype(jnp.float32)
            squared = jnp.sum(wide * wide, axis=1, keepdims=True)
            out_ref[...] = (wide * lax.rsqrt(squared + 1e-06)).astype(jnp.bfloat16)

        return body

    return call


def products_kernel(plan, n_own, n_far, n_near, *refs):
    refs = list(refs)
    own_tag, far_tag, near_tag = refs[:3]
    state_in = refs[3:6]
    chunks = refs[6 : 6 + n_own + n_far + n_near]
    state_out = refs[6 + n_own + n_far + n_near : 9 + n_own + n_far + n_near]
    racc, cacc = refs[-2:]
    rows, cols, pairs, block = plan
    near_tags = near_tag[...].astype(jnp.float32)
    near_tags = jnp.where(near_tags < 0.0, -2.0, near_tags)
    row_tags = (own_tag[...].astype(jnp.float32), far_tag[...].astype(jnp.float32))
    cacc[...] = jnp.full(cacc.shape, -1.0, jnp.float32)
    col_base = [sum(size for _, _, size in cols[:i]) for i in range(len(cols))]
    for old, new in zip(state_in, state_out):
        new[...] = old[...]
    for r, (which, ref, start, size) in enumerate(rows):
        mine = [c for c in range(len(cols)) if (r, c) in pairs]
        for i in range(0, size, block):
            height = min(block, size - i)
            left = chunks[ref][i : i + height, :]
            tag = []
            for q in range(0, height, LANES):
                line = row_tags[which][(start + i + q) // LANES][None, :]
                tag.append(jnp.broadcast_to(line, (LANES, LANES)).T)
            tag = jnp.concatenate(tag, axis=0)
            best = jnp.full((height, LANES), -1.0, jnp.float32)
            for c in mine:
                col_ref, col_start, col_size = cols[c]
                for j in range(0, col_size, block):
                    width = min(block, col_size - j)
                    right = chunks[col_ref][j : j + width, :]
                    tile = lax.dot_general(
                        left, right, (((1,), (1,)), ((), ())), preferred_element_type=jnp.float32
                    )
                    for g in range(0, width, LANES):
                        line = near_tags[(col_start + j + g) // LANES][None, :]
                        part = jnp.where(tag == line, tile[:, g : g + LANES], -1.0)
                        best = jnp.maximum(best, part)
                        at = col_base[c] + j + g
                        high = jnp.max(part.reshape(height // 8, 8, LANES), axis=0)
                        cacc[:, at : at + LANES] = jnp.maximum(cacc[:, at : at + LANES], high)
            racc[0:height, :] = best
            for q in range(0, height, LANES):
                line = jnp.max(racc[q : q + LANES, :].T, axis=0, keepdims=True)
                at = (start + i + q) // LANES
                state_out[which][at : at + 1, :] = jnp.maximum(state_out[which][at : at + 1, :], line)
    for c, (_, col_start, col_size) in enumerate(cols):
        for j in range(0, col_size, LANES):
            at = col_base[c] + j
            line = jnp.max(cacc[:, at : at + LANES], axis=0, keepdims=True)
            at = (col_start + j) // LANES
            state_out[2][at : at + 1, :] = jnp.maximum(state_out[2][at : at + 1, :], line)


def products(state, tags, own, far, near, want, sizes, block=512):
    starts = [sum(sizes[:i]) for i in range(len(sizes))]
    row_keys = sorted({(w, r) for w, r, _ in want})
    col_keys = sorted({c for _, _, c in want})
    operands, rows, cols = [], [], []
    for which, r in row_keys:
        rows.append((which, len(operands), starts[r], sizes[r]))
        operands.append((own, far)[which][r])
    for c in col_keys:
        cols.append((len(operands), starts[c], sizes[c]))
        operands.append(near[c])
    pairs = frozenset((row_keys.index((w, r)), col_keys.index(c)) for w, r, c in want)
    plan = (tuple(rows), tuple(cols), pairs, block)
    whole = pl.BlockSpec(memory_space=pltpu.VMEM)
    depth = operands[0].shape[1]
    tag_spec = pl.BlockSpec((TAG_ROWS, LANES), lambda i: (sizes[0] // TAG_ROWS, 0))
    data_specs = [pl.BlockSpec(o.shape, lambda i: (0, 0)) for o in operands]
    state_spec = [pl.BlockSpec(s.shape, lambda i: (0, 0)) for s in state]
    macs = sum(sizes[r] * sizes[c] for _, r, c in want)
    kernel = functools.partial(products_kernel, plan, len(operands), 0, 0)
    return pl.pallas_call(
        kernel,
        grid=(1,),
        in_specs=[tag_spec] * 3 + state_spec + data_specs,
        out_specs=state_spec,
        out_shape=[jax.ShapeDtypeStruct(s.shape, s.dtype) for s in state],
        scratch_shapes=[
            pltpu.VMEM((block, LANES), jnp.float32),
            pltpu.VMEM((8, sum(size for _, _, size in cols)), jnp.float32),
        ],
        compiler_params=pltpu.CompilerParams(vmem_limit_bytes=32 << 20),
        cost_estimate=pl.CostEstimate(flops=2 * macs * depth, bytes_accessed=2 * depth * 4096, transcendentals=0),
        name="products",
    )(*tags, *state, *operands)


def per_device(embeddings, cluster_ids, row_counts, *, near_route, far_route):
    rows = embeddings.shape[0]
    sizes = CHUNKS
    back_route = [(b, a) for a, b in near_route]
    ids = cluster_ids.reshape(rows // LANES, LANES)
    own = [normalize(True, 0, sizes[0])(embeddings, row_counts, ids)]
    near = [lax.ppermute(own[0], AXES, near_route)]
    far = [lax.ppermute(own[0], AXES, far_route)]
    start = sizes[0]
    for size in sizes[1:]:
        own.append(normalize(False, start, size)(embeddings))
        near.append(lax.ppermute(own[-1], AXES, near_route))
        far.append(lax.ppermute(own[-1], AXES, far_route))
        start += size
    state = [jnp.full((rows // LANES, LANES), -1.0, jnp.float32)] * 3
    tags = (own[0], far[0], near[0])
    last = len(sizes) - 1
    every = range(len(sizes))
    fold = functools.partial(products, own=own, far=far, near=near, sizes=sizes)
    for c in every:
        want = {(0, r, c) for r in every}
        if c < last:
            want |= {(1, r, c) for r in range(c + 1)}
            want |= {(1, c, k) for k in range(c)}
        else:
            want |= {(1, r, c) for r in range(c)}
        state = fold(state, tags, want=want)
    state = fold(state, tags, want={(1, last, k) for k in every})
    kept, far_best, near_best = [s.reshape(rows) for s in state]
    from_near = lax.ppermute(near_best, AXES, back_route)
    from_far = lax.ppermute(far_best, AXES, far_route)
    return jnp.maximum(kept, jnp.maximum(from_near, from_far))


def solution(mesh):
    near_route, far_route = routes(mesh.shape["grp"], mesh.shape["pair"])
    return jax.shard_map(
        functools.partial(per_device, near_route=near_route, far_route=far_route),
        mesh=mesh,
        in_specs=(P(("grp", "pair"), None), P(("grp", "pair")), P(("grp", "pair"))),
        out_specs=P(("grp", "pair")),
        check_vma=False,
    )
```

time: 161 us -> 64.4 us (0.40); the launches traced: 158 us -> 63.8 us
  waiting for transfers between devices: 95.4 us -> 14.7 us
  Pallas kernels: 0 us -> 20.4 us
  matrix products: 17 us -> 0 us
  starting transfers between devices: 39.5 us -> 25 us
  other arithmetic: 3.44 us -> 0.6 us
    ppermute x12 -> x8, waiting for transfers between devices: 95.4 us -> 14.7 us  [the longest x1 9.88 us: per_device(): far = [lax.ppermute(own[0], AXES, far_route)]]
    pallas_call x0 -> x7, Pallas kernels: none -> 20.4 us  [the longest x4 12.8 us: products(): pl.pallas_call(kernel, grid=(1,), in_specs=[tag_spec] * 3 + state_spec +...]
    dot_general x4 -> x0, matrix products: 17 us -> none  [masked_max(): lax.dot_general(left, right, (((1,), (1,)), ((), ())), preferred_element_...]
    ppermute x12 -> x8, starting transfers between devices: 39.5 us -> 25 us  [the longest x2 12.9 us: per_device(): far.append(lax.ppermute(own[-1], AXES, far_route))]
    reduce_sum x1 -> x0, other arithmetic: 2.34 us -> none  [per_device(): squared = jnp.sum(wide * wide, axis=1, keepdims=True)]
  transfers between devices with their start and end apart: 12 -> 8, of which waited for: 3 -> 3; matrix products, arithmetic and copies ran while one was open for 11% -> 0% of each run, Pallas kernels for 0% -> 23%
where the time goes in v1:
time: 64.4 us; the launch traced here: 63.8 us
  starting transfers between devices  25 us (39%)
  Pallas kernels  20.4 us (32%)
  waiting for transfers between devices  14.7 us (23%)
  local copies, waits for them, and re-layouts  2.27 us (4%)
  between operations  0.8 us (1%)
    ppermute x2, starting transfers between devices, per_device(): far.append(lax.ppermute(own[-1], AXES, far_route))  12.9 us
    pallas_call x4, Pallas kernels, products(): pl.pallas_call(kernel, grid=(1,), in_specs=[tag_spec] * 3 + state_spec +...  12.8 us
    ppermute x1, waiting for transfers between devices, per_device(): far = [lax.ppermute(own[0], AXES, far_route)]  9.88 us
    pallas_call x3, Pallas kernels, call(): pl.pallas_call(kernel if tagged else kernel_of_step(step), grid=(count //...  7.58 us
    ppermute x2, starting transfers between devices, per_device(): near.append(lax.ppermute(own[-1], AXES, near_route))  4.33 us
    ppermute x1, waiting for transfers between devices, per_device(): from_far = lax.ppermute(far_best, AXES, far_route)  3.14 us
    unnamed x10, local copies, waits for them, and re-layouts  2.27 us
    ppermute x1, starting transfers between devices, per_device(): far = [lax.ppermute(own[0], AXES, far_route)]  2.04 us
  transfers between devices with their start and end apart: 8, of which 3 were waited for; matrix products, arithmetic and copies ran while one was open for 0% of the time, Pallas kernels for 23%

profile of v1, /device:TPU:6, one launch (start us, length us, event | category | flops | bytes accessed | tf_op | source)
XLA Modules:
  0.0 63.8 jit_solution(2190057113309451179)
XLA Ops:
  0.0 3.4 %normalize.4.refs_7_ = bf16[768,768]{1,0:T(8,128)(2,1)} custom-call(bf16[1536,768]{1,0:T(8,128)(2,1)} %rows_ref.3), custom_call_target="tpu_custom_call" | custom-call | flops 2359296 | bytes 2359296 | tf_op jit(solution)/shard_map/normalize/pallas_call | solution.py:64
  3.4 7.7 %collective-permute-start.2 = (bf16[768,768]{1,0:T(8,128)(2,1)}, bf16[768,768]{1,0:T(8,128)(2,1)}, u32[]{:S(2)}, u32[]{:S(2)}) collective-permute-start(bf16[768,768]{1,0:T(8,128)(2,1)} %normalize.4.refs_7_), channel_id=1, source_target_pairs={{0,12},{1,13},{2,14},{3,15},{4,52},{5,53},{6,54},{7,55},{8,56},{9,... | collective-permute-start | bytes 3538952 | tf_op jit(solution)/shard_map/ppermute | solution.py:187
  11.1 1.9 %collective-permute-start.3 = (bf16[768,768]{1,0:T(8,128)(2,1)}, bf16[768,768]{1,0:T(8,128)(2,1)}, u32[]{:S(2)}, u32[]{:S(2)}) collective-permute-start(bf16[768,768]{1,0:T(8,128)(2,1)} %normalize.4.refs_7_), channel_id=1, source_target_pairs={{0,16},{1,17},{2,18},{3,19},{4,0},{5,1},{6,2},{7,3},{8,12},{9,13},... | collective-permute-start | bytes 3538952 | tf_op jit(solution)/shard_map/ppermute | solution.py:186
  13.7 2.3 %normalize.3.refs_0_.refs_6_ = bf16[528,768]{1,0:T(8,128)(2,1)} custom-call(s32[1]{0:T(128)S(6)} %copy.4.refs_0_, s32[12,128]{1,0:T(8,128)} %bitcast.7, bf16[1536,768]{1,0:T(8,128)(2,1)} %rows_ref.3), custom_call_target="tpu_custom_call" | custom-call | flops 1572864 | bytes 1572864 | tf_op jit(solution)/shard_map/normalize/pallas_call | solution.py:64
  16.0 0.0 copy-start
  16.0 2.0 %collective-permute-start = (bf16[528,768]{1,0:T(8,128)(2,1)}, bf16[528,768]{1,0:T(8,128)(2,1)S(1)}, u32[]{:S(2)}, u32[]{:S(2)}) collective-permute-start(bf16[528,768]{1,0:T(8,128)(2,1)} %normalize.3.refs_0_.refs_6_), channel_id=1, source_target_pairs={{0,12},{1,13},{2,14},{3,15},{4,52},{5,53},{6,54},{7,55},{8,56},{9,... | collective-permute-start | bytes 2433032 | tf_op jit(solution)/shard_map/ppermute | solution.py:182
  18.0 1.9 %collective-permute-start.1 = (bf16[528,768]{1,0:T(8,128)(2,1)}, bf16[528,768]{1,0:T(8,128)(2,1)S(1)}, u32[]{:S(2)}, u32[]{:S(2)}) collective-permute-start(bf16[528,768]{1,0:T(8,128)(2,1)} %normalize.3.refs_0_.refs_6_), channel_id=1, source_target_pairs={{0,16},{1,17},{2,18},{3,19},{4,0},{5,1},{6,2},{7,3},{8,12},{9,13},... | collective-permute-start | bytes 2433032 | tf_op jit(solution)/shard_map/ppermute | solution.py:181
  20.0 1.9 %normalize.5.refs_8_ = bf16[256,768]{1,0:T(8,128)(2,1)} custom-call(bf16[1536,768]{1,0:T(8,128)(2,1)} %rows_ref.3), custom_call_target="tpu_custom_call" | custom-call | flops 786432 | bytes 786432 | tf_op jit(solution)/shard_map/normalize/pallas_call | solution.py:64
  21.9 2.4 %collective-permute-start.4 = (bf16[256,768]{1,0:T(8,128)(2,1)}, bf16[256,768]{1,0:T(8,128)(2,1)S(1)}, u32[]{:S(2)}, u32[]{:S(2)}) collective-permute-start(bf16[256,768]{1,0:T(8,128)(2,1)} %normalize.5.refs_8_), channel_id=1, source_target_pairs={{0,16},{1,17},{2,18},{3,19},{4,0},{5,1},{6,2},{7,3},{8,12},{9,13},... | collective-permute-start | bytes 1179656 | tf_op jit(solution)/shard_map/ppermute | solution.py:186
  24.3 9.9 %collective-permute-done.refs_1_.refs_9_ = bf16[528,768]{1,0:T(8,128)(2,1)S(1)} collective-permute-done((bf16[528,768]{1,0:T(8,128)(2,1)}, bf16[528,768]{1,0:T(8,128)(2,1)S(1)}, u32[]{:S(2)}, u32[]{:S(2)}) %collective-permute-start) | collective-permute-done | bytes 811040 | tf_op jit(solution)/shard_map/ppermute | solution.py:182
  34.2 5.1 %collective-permute-start.5 = (bf16[256,768]{1,0:T(8,128)(2,1)}, bf16[256,768]{1,0:T(8,128)(2,1)S(1)}, u32[]{:S(2)}, u32[]{:S(2)}) collective-permute-start(bf16[256,768]{1,0:T(8,128)(2,1)} %normalize.5.refs_8_), channel_id=1, source_target_pairs={{0,12},{1,13},{2,14},{3,15},{4,52},{5,53},{6,54},{7,55},{8,56},{9,... | collective-permute-start | bytes 1179656 | tf_op jit(solution)/shard_map/ppermute | solution.py:187
  39.3 0.0 collective-permute-done.1.refs_2_.refs_10_.refs_11_.refs_7_
  39.3 0.0 copy-done
  39.4 0.0 copy-start.1
  39.4 1.3 %copy-done.1 = bf16[768,768]{1,0:T(8,128)(2,1)S(1)} copy-done((bf16[768,768]{1,0:T(8,128)(2,1)S(1)}, bf16[768,768]{1,0:T(8,128)(2,1)}, u32[]{:S(2)}) %copy-start.1) | copy-done | bytes 1179672
  40.6 0.0 copy-start.3
  40.6 1.0 %copy-done.3 = bf16[256,768]{1,0:T(8,128)(2,1)S(1)} copy-done((bf16[256,768]{1,0:T(8,128)(2,1)S(1)}, bf16[256,768]{1,0:T(8,128)(2,1)}, u32[]{:S(2)}) %copy-start.3) | copy-done | bytes 393240
  41.6 1.9 %products.4 = (f32[12,128]{1,0:T(8,128)S(1)}, f32[12,128]{1,0:T(8,128)S(1)}, f32[12,128]{1,0:T(8,128)S(1)}) custom-call(bf16[528,768]{1,0:T(8,128)(2,1)S(1)} %copy-done, bf16[528,768]{1,0:T(8,128)(2,1)S(1)} %collective-permute-done.refs_1_.refs_9_, bf16[528,768]{1,0:T(8,128)(2,1)S(1)} %collective-permute-done.1.refs_2_.refs_10_.refs_11_.refs_7_, ...), custom_call_target="tpu_custom_call" | custom-call | flops 1610612736 | bytes 6291456 | tf_op jit(solution)/shard_map/products/pallas_call | solution.py:159
  43.5 0.0 collective-permute-done.2.refs_10_
  43.6 0.0 collective-permute-done.3.refs_12_.refs_8_
  43.6 0.0 copy-done.2
  43.6 0.0 copy-done.4
  43.6 6.0 %products.5 = (f32[12,128]{1,0:T(8,128)S(1)}, f32[12,128]{1,0:T(8,128)S(1)}, f32[12,128]{1,0:T(8,128)S(1)}) custom-call(bf16[528,768]{1,0:T(8,128)(2,1)S(1)} %copy-done, bf16[528,768]{1,0:T(8,128)(2,1)S(1)} %collective-permute-done.refs_1_.refs_9_, bf16[528,768]{1,0:T(8,128)(2,1)S(1)} %collective-permute-done.1.refs_2_.refs_10_.refs_11_.refs_7_, ...), custom_call_target="tpu_custom_call" | custom-call | flops 3925868544 | bytes 6291456 | tf_op jit(solution)/shard_map/products/pallas_call | solution.py:159
  49.6 0.0 collective-permute-done.4.refs_11_.refs_9_
  49.6 2.8 %products.6 = (f32[12,128]{1,0:T(8,128)S(1)}, f32[12,128]{1,0:T(8,128)S(1)}, f32[12,128]{1,0:T(8,128)S(1)}) custom-call(bf16[528,768]{1,0:T(8,128)(2,1)S(1)} %copy-done, bf16[528,768]{1,0:T(8,128)(2,1)S(1)} %collective-permute-done.refs_1_.refs_9_, bf16[528,768]{1,0:T(8,128)(2,1)S(1)} %collective-permute-done.1.refs_2_.refs_10_.refs_11_.refs_7_, ...), custom_call_target="tpu_custom_call" | custom-call | flops 1107296256 | bytes 6291456 | tf_op jit(solution)/shard_map/products/pallas_call | solution.py:159
  52.4 0.0 collective-permute-done.5.refs_6_
  52.4 2.2 %products.7 = (f32[12,128]{1,0:T(8,128)S(1)}, f32[12,128]{1,0:T(8,128)S(1)}, f32[12,128]{1,0:T(8,128)S(1)}) custom-call(bf16[528,768]{1,0:T(8,128)(2,1)S(1)} %copy-done, bf16[528,768]{1,0:T(8,128)(2,1)S(1)} %collective-permute-done.refs_1_.refs_9_, bf16[528,768]{1,0:T(8,128)(2,1)S(1)} %collective-permute-done.1.refs_2_.refs_10_.refs_11_.refs_7_, ...), custom_call_target="tpu_custom_call" | custom-call | flops 603979776 | bytes 6291456 | tf_op jit(solution)/shard_map/products/pallas_call | solution.py:159
  54.5 1.9 %collective-permute-start.6 = (f32[1536]{0:T(1024)S(1)}, f32[1536]{0:T(1024)S(1)}, u32[]{:S(2)}, u32[]{:S(2)}) collective-permute-start(f32[1536]{0:T(1024)S(1)} %bitcast.6), channel_id=1, source_target_pairs={{16,0},{17,1},{18,2},{19,3},{0,4},{1,5},{2,6},{3,7},{12,8},{13,9},... | collective-permute-start | bytes 18440 | tf_op jit(solution)/shard_map/ppermute | solution.py:204
  56.5 1.9 %collective-permute-start.7 = (f32[1536]{0:T(1024)S(1)}, f32[1536]{0:T(1024)S(1)}, u32[]{:S(2)}, u32[]{:S(2)}) collective-permute-start(f32[1536]{0:T(1024)S(1)} %bitcast.5), channel_id=1, source_target_pairs={{0,12},{1,13},{2,14},{3,15},{4,52},{5,53},{6,54},{7,55},{8,56},{9,... | collective-permute-start | bytes 18440 | tf_op jit(solution)/shard_map/ppermute | solution.py:205
  58.4 1.7 %collective-permute-done.6 = f32[1536]{0:T(1024)S(1)} collective-permute-done((f32[1536]{0:T(1024)S(1)}, f32[1536]{0:T(1024)S(1)}, u32[]{:S(2)}, u32[]{:S(2)}) %collective-permute-start.6) | collective-permute-done | bytes 6176 | tf_op jit(solution)/shard_map/ppermute | solution.py:204
  60.1 3.1 %collective-permute-done.7 = f32[1536]{0:T(1024)S(1)} collective-permute-done((f32[1536]{0:T(1024)S(1)}, f32[1536]{0:T(1024)S(1)}, u32[]{:S(2)}, u32[]{:S(2)}) %collective-permute-start.7) | collective-permute-done | bytes 6176 | tf_op jit(solution)/shard_map/ppermute | solution.py:205
  63.2 0.6 bitcast_maximum_fusion
  (3 shorter events, 0.0 us)
Async XLA Ops:
  3.4 40.2 %collective-permute-start.2 = (bf16[768,768]{1,0:T(8,128)(2,1)}, bf16[768,768]{1,0:T(8,128)(2,1)}, u32[]{:S(2)}, u32[]{:S(2)}) collective-permute-start(bf16[768,768]{1,0:T(8,128)(2,1)} %normalize.4.refs_7_), channel_id=1, source_target_pairs={{0,12},{1,13},{2,14},{3,15},{4,52},{5,53},{6,54},{7,55},{8,56},{9,... | collective-permute-start | bytes 3538952 | tf_op jit(solution)/shard_map/ppermute | solution.py:187
  11.1 32.4 %collective-permute-start.3 = (bf16[768,768]{1,0:T(8,128)(2,1)}, bf16[768,768]{1,0:T(8,128)(2,1)}, u32[]{:S(2)}, u32[]{:S(2)}) collective-permute-start(bf16[768,768]{1,0:T(8,128)(2,1)} %normalize.4.refs_7_), channel_id=1, source_target_pairs={{0,16},{1,17},{2,18},{3,19},{4,0},{5,1},{6,2},{7,3},{8,12},{9,13},... | collective-permute-start | bytes 3538952 | tf_op jit(solution)/shard_map/ppermute | solution.py:186
  16.0 23.4 %copy-start = (bf16[528,768]{1,0:T(8,128)(2,1)S(1)}, bf16[528,768]{1,0:T(8,128)(2,1)}, u32[]{:S(2)}) copy-start(bf16[528,768]{1,0:T(8,128)(2,1)} %normalize.3.refs_0_.refs_6_) | copy-start | bytes 2433028
  16.0 18.2 %collective-permute-start = (bf16[528,768]{1,0:T(8,128)(2,1)}, bf16[528,768]{1,0:T(8,128)(2,1)S(1)}, u32[]{:S(2)}, u32[]{:S(2)}) collective-permute-start(bf16[528,768]{1,0:T(8,128)(2,1)} %normalize.3.refs_0_.refs_6_), channel_id=1, source_target_pairs={{0,12},{1,13},{2,14},{3,15},{4,52},{5,53},{6,54},{7,55},{8,56},{9,... | collective-permute-start | bytes 2433032 | tf_op jit(solution)/shard_map/ppermute | solution.py:182
  18.0 21.3 %collective-permute-start.1 = (bf16[528,768]{1,0:T(8,128)(2,1)}, bf16[528,768]{1,0:T(8,128)(2,1)S(1)}, u32[]{:S(2)}, u32[]{:S(2)}) collective-permute-start(bf16[528,768]{1,0:T(8,128)(2,1)} %normalize.3.refs_0_.refs_6_), channel_id=1, source_target_pairs={{0,16},{1,17},{2,18},{3,19},{4,0},{5,1},{6,2},{7,3},{8,12},{9,13},... | collective-permute-start | bytes 2433032 | tf_op jit(solution)/shard_map/ppermute | solution.py:181
  21.9 27.7 %collective-permute-start.4 = (bf16[256,768]{1,0:T(8,128)(2,1)}, bf16[256,768]{1,0:T(8,128)(2,1)S(1)}, u32[]{:S(2)}, u32[]{:S(2)}) collective-permute-start(bf16[256,768]{1,0:T(8,128)(2,1)} %normalize.5.refs_8_), channel_id=1, source_target_pairs={{0,16},{1,17},{2,18},{3,19},{4,0},{5,1},{6,2},{7,3},{8,12},{9,13},... | collective-permute-start | bytes 1179656 | tf_op jit(solution)/shard_map/ppermute | solution.py:186
  34.2 18.2 %collective-permute-start.5 = (bf16[256,768]{1,0:T(8,128)(2,1)}, bf16[256,768]{1,0:T(8,128)(2,1)S(1)}, u32[]{:S(2)}, u32[]{:S(2)}) collective-permute-start(bf16[256,768]{1,0:T(8,128)(2,1)} %normalize.5.refs_8_), channel_id=1, source_target_pairs={{0,12},{1,13},{2,14},{3,15},{4,52},{5,53},{6,54},{7,55},{8,56},{9,... | collective-permute-start | bytes 1179656 | tf_op jit(solution)/shard_map/ppermute | solution.py:187
  39.4 1.3 %copy-start.1 = (bf16[768,768]{1,0:T(8,128)(2,1)S(1)}, bf16[768,768]{1,0:T(8,128)(2,1)}, u32[]{:S(2)}) copy-start(bf16[768,768]{1,0:T(8,128)(2,1)} %normalize.4.refs_7_) | copy-start | bytes 3538948
  40.6 1.0 %copy-start.3 = (bf16[256,768]{1,0:T(8,128)(2,1)S(1)}, bf16[256,768]{1,0:T(8,128)(2,1)}, u32[]{:S(2)}) copy-start(bf16[256,768]{1,0:T(8,128)(2,1)} %normalize.5.refs_8_) | copy-start | bytes 1179652
  41.6 1.9 %copy-start.2 = (bf16[768,768]{1,0:T(8,128)(2,1)S(1)}, bf16[768,768]{1,0:T(8,128)(2,1)}, u32[]{:S(2)}) copy-start(bf16[768,768]{1,0:T(8,128)(2,1)} %normalize.4.refs_7_) | copy-start | bytes 3538948
  41.6 2.0 %copy-start.4 = (bf16[256,768]{1,0:T(8,128)(2,1)S(1)}, bf16[256,768]{1,0:T(8,128)(2,1)}, u32[]{:S(2)}) copy-start(bf16[256,768]{1,0:T(8,128)(2,1)} %normalize.5.refs_8_) | copy-start | bytes 1179652
  54.5 5.5 %collective-permute-start.6 = (f32[1536]{0:T(1024)S(1)}, f32[1536]{0:T(1024)S(1)}, u32[]{:S(2)}, u32[]{:S(2)}) collective-permute-start(f32[1536]{0:T(1024)S(1)} %bitcast.6), channel_id=1, source_target_pairs={{16,0},{17,1},{18,2},{19,3},{0,4},{1,5},{2,6},{3,7},{12,8},{13,9},... | collective-permute-start | bytes 18440 | tf_op jit(solution)/shard_map/ppermute | solution.py:204
  56.5 6.8 %collective-permute-start.7 = (f32[1536]{0:T(1024)S(1)}, f32[1536]{0:T(1024)S(1)}, u32[]{:S(2)}, u32[]{:S(2)}) collective-permute-start(f32[1536]{0:T(1024)S(1)} %bitcast.5), channel_id=1, source_target_pairs={{0,12},{1,13},{2,14},{3,15},{4,52},{5,53},{6,54},{7,55},{8,56},{9,... | collective-permute-start | bytes 18440 | tf_op jit(solution)/shard_map/ppermute | solution.py:205

commit v2 on v1

v2 whole, which is shorter than its diff:
```python
import functools

import jax
import jax.numpy as jnp
from jax import lax
from jax.experimental import pallas as pl
from jax.experimental.pallas import tpu as pltpu
from jax.sharding import PartitionSpec as P

LANES = 128
TAG_ROWS = 16
CHUNKS = (768, 512, 256)
AXES = ("grp", "pair")


def routes(grp, pair):
    side = 4
    rest = pair // (side * side)
    near, far = [], []
    for g in range(grp):
        for y in range(side):
            for x in range(side):
                for z in range(rest):

                    def at(v, u):
                        return g * pair + (v * side + u) * rest + z

                    owns_y = (y in (1, 2)) ^ (x in (1, 2)) ^ (g % 2 == 1)
                    here = at(y, x)
                    near.append((here, at(y, x ^ 1) if owns_y else at(y ^ 1, x)))
                    far.append((here, at(3 - y, x) if owns_y else at(y, 3 - x)))
    return near, far


def normalize(rows, first, count, step, row_counts=None, ids=None):
    width = rows.shape[1]
    tagged = ids is not None
    places = [(at, min(step, count - at)) for at in range(0, count, step)]

    def kernel(*refs):
        rows_ref, out_ref, held, arrived = refs[:1] + refs[1 + 2 * tagged : 4 + 2 * tagged]
        copies = [
            pltpu.make_async_copy(rows_ref.at[pl.ds(first + at, size)], held.at[pl.ds(at, size)], arrived.at[i])
            for i, (at, size) in enumerate(places)
        ]
        if tagged:
            valid_ref, ids_ref = refs[1:3]
            held_ids = refs[6]
            ids_copy = pltpu.make_async_copy(ids_ref, held_ids, arrived.at[len(places)])
            ids_copy.start()
        for copy in copies:
            copy.start()
        for copy, (at, size) in zip(copies, places):
            copy.wait()
            wide = held[at : at + size, :].astype(jnp.float32)
            squared = jnp.sum(wide * wide, axis=1, keepdims=True)
            out_ref[at : at + size, :] = (wide * lax.rsqrt(squared + 1e-06)).astype(jnp.bfloat16)
        if tagged:
            ids_copy.wait()
            ids = held_ids[...]
            place = lax.broadcasted_iota(jnp.int32, ids.shape, 0) * LANES
            place = place + lax.broadcasted_iota(jnp.int32, ids.shape, 1)
            tags = jnp.where(place < valid_ref[0], ids, -1).astype(jnp.float32)
            spare = jnp.full((TAG_ROWS - ids.shape[0], LANES), -1.0, jnp.float32)
            out_ref[count:, 0:LANES] = jnp.concatenate([tags, spare], axis=0).astype(jnp.bfloat16)
            out_ref[count:, LANES:] = jnp.zeros((TAG_ROWS, width - LANES), jnp.bfloat16)

    in_hbm = pl.BlockSpec(memory_space=pltpu.HBM)
    total = count + (TAG_ROWS if tagged else 0)
    scratch = [pltpu.VMEM((count, width), jnp.bfloat16), pltpu.SemaphoreType.DMA((len(places) + 1,))]
    if tagged:
        scratch += [pltpu.VMEM(ids.shape, jnp.int32)]
    operands = [pltpu.with_memory_space_constraint(rows, pltpu.HBM)]
    if tagged:
        operands += [row_counts, pltpu.with_memory_space_constraint(ids, pltpu.HBM)]
    return pl.pallas_call(
        kernel,
        in_specs=[in_hbm, pl.BlockSpec(memory_space=pltpu.SMEM), in_hbm] if tagged else [in_hbm],
        out_specs=pl.BlockSpec(memory_space=pltpu.VMEM),
        out_shape=pltpu.VMEM((total, width), jnp.bfloat16),
        scratch_shapes=scratch,
        compiler_params=pltpu.CompilerParams(vmem_limit_bytes=16 << 20),
        cost_estimate=pl.CostEstimate(flops=4 * count * width, bytes_accessed=4 * count * width, transcendentals=count),
        name="normalize",
    )(*operands)


def products_kernel(plan, *refs):
    rows, cols, pairs, touched, tag_at, block, n_chunks = plan
    state_in = dict(zip(touched, refs[: len(touched)]))
    refs = refs[len(touched) :]
    chunks = refs[:n_chunks]
    state_out = dict(zip(touched, refs[n_chunks : n_chunks + len(touched)]))
    cacc = refs[-1]

    def tags_of(which):
        ref, at = tag_at[which]
        return chunks[ref][at : at + TAG_ROWS, 0:LANES].astype(jnp.float32)

    near_tags = tags_of(2)
    near_tags = jnp.where(near_tags < 0.0, -2.0, near_tags)
    row_tags = {which: tags_of(which) for which in {row[0] for row in rows}}
    cacc[...] = jnp.full(cacc.shape, -1.0, jnp.float32)
    for key in touched:
        state_out[key][...] = state_in[key][...]
    for r, (which, ref, start, size) in enumerate(rows):
        mine = [c for c in range(len(cols)) if (r, c) in pairs]
        for i in range(0, size, block):
            height = min(block, size - i)
            left = chunks[ref][i : i + height, :]
            tag = []
            for q in range(0, height, LANES):
                line = row_tags[which][(start + i + q) // LANES][None, :]
                tag.append(jnp.broadcast_to(line, (LANES, LANES)).T)
            tag = jnp.concatenate(tag, axis=0)
            best = jnp.full((height, LANES), -1.0, jnp.float32)
            for c in mine:
                col_ref, col_start, col_size, base = cols[c]
                for j in range(0, col_size, block):
                    width = min(block, col_size - j)
                    right = chunks[col_ref][j : j + width, :]
                    tile = lax.dot_general(
                        left, right, (((1,), (1,)), ((), ())), preferred_element_type=jnp.float32
                    )
                    for g in range(0, width, LANES):
                        line = near_tags[(col_start + j + g) // LANES][None, :]
                        part = jnp.where(tag == line, tile[:, g : g + LANES], -1.0)
                        best = jnp.maximum(best, part)
                        at = base + j + g
                        high = jnp.max(part.reshape(height // 8, 8, LANES), axis=0)
                        cacc[:, at : at + LANES] = jnp.maximum(cacc[:, at : at + LANES], high)
            for q in range(0, height, LANES):
                line = jnp.max(best[q : q + LANES, :].T, axis=0, keepdims=True)
                at = (start + i + q) // LANES
                state_out[which][at : at + 1, :] = jnp.maximum(state_out[which][at : at + 1, :], line)
    for _, col_start, col_size, base in cols:
        for j in range(0, col_size, LANES):
            line = jnp.max(cacc[:, base + j : base + j + LANES], axis=0, keepdims=True)
            at = (col_start + j) // LANES
            state_out[2][at : at + 1, :] = jnp.maximum(state_out[2][at : at + 1, :], line)


def products(state, own, far, near, want, sizes, block=512):
    arrays = (own, far, near)
    starts = [sum(sizes[:i]) for i in range(len(sizes))]
    row_keys = sorted({(w, r) for w, r, _ in want})
    col_keys = sorted({c for _, _, c in want})
    touched = tuple(sorted({w for w, _ in row_keys} | {2}))
    keys = row_keys + [(2, c) for c in col_keys]
    keys += [(w, 0) for w in touched if (w, 0) not in keys]
    rows = tuple((w, keys.index((w, r)), starts[r], sizes[r]) for w, r in row_keys)
    cols = tuple(
        (keys.index((2, c)), starts[c], sizes[c], sum(sizes[k] for k in col_keys[:i])) for i, c in enumerate(col_keys)
    )
    pairs = frozenset((row_keys.index((w, r)), col_keys.index(c)) for w, r, c in want)
    tag_at = {w: (keys.index((w, 0)), sizes[0]) for w in touched}
    plan = (rows, cols, pairs, touched, tag_at, block, len(keys))
    operands = [pltpu.with_memory_space_constraint(arrays[w][c], pltpu.VMEM) for w, c in keys]
    before = [state[w] for w in touched]
    depth = operands[0].shape[1]
    whole = pl.BlockSpec(memory_space=pltpu.VMEM)
    macs = sum(sizes[r] * sizes[c] for _, r, c in want)
    after = pl.pallas_call(
        functools.partial(products_kernel, plan),
        in_specs=[whole] * (len(before) + len(operands)),
        out_specs=[whole] * len(before),
        out_shape=[jax.ShapeDtypeStruct(s.shape, s.dtype) for s in before],
        scratch_shapes=[pltpu.VMEM((8, sum(sizes[c] for c in col_keys)), jnp.float32)],
        compiler_params=pltpu.CompilerParams(vmem_limit_bytes=16 << 20),
        cost_estimate=pl.CostEstimate(flops=2 * macs * depth, bytes_accessed=2 * macs, transcendentals=0),
        name="products",
    )(*before, *operands)
    state = list(state)
    for w, value in zip(touched, after):
        state[w] = value
    return state


def per_device(embeddings, cluster_ids, row_counts, *, near_route, far_route):
    rows = embeddings.shape[0]
    sizes = CHUNKS
    back_route = [(b, a) for a, b in near_route]
    ids = cluster_ids.reshape(rows // LANES, LANES)
    own = [normalize(embeddings, 0, sizes[0], 256, row_counts, ids)]
    far = [lax.ppermute(own[0], AXES, far_route)]
    near = [lax.ppermute(own[0], AXES, near_route)]
    start = sizes[0]
    for size in sizes[1:]:
        embeddings, own[-1] = lax.optimization_barrier((embeddings, own[-1]))
        own.append(normalize(embeddings, start, size, 256))
        far.append(lax.ppermute(own[-1], AXES, far_route))
        near.append(lax.ppermute(own[-1], AXES, near_route))
        start += size
    state = [jnp.full((rows // LANES, LANES), -1.0, jnp.float32)] * 3
    last = len(sizes) - 1
    every = range(len(sizes))
    fold = functools.partial(products, own=own, far=far, near=near, sizes=sizes)
    state = fold(state, want={(0, r, 0) for r in every} | {(1, 0, 0)})
    for c in range(1, last):
        state = fold(state, want={(1, c, k) for k in range(c)})
        state = fold(state, want={(0, r, c) for r in every} | {(1, r, c) for r in range(c + 1)})
    state = fold(state, want={(1, last, k) for k in range(last)})
    state = fold(state, want={(0, r, last) for r in every} | {(1, r, last) for r in every})
    kept, far_best, near_best = [s.reshape(rows) for s in state]
    from_near = lax.ppermute(near_best, AXES, back_route)
    from_far = lax.ppermute(far_best, AXES, far_route)
    return jnp.maximum(kept, jnp.maximum(from_near, from_far))


def solution(mesh):
    near_route, far_route = routes(mesh.shape["grp"], mesh.shape["pair"])
    return jax.shard_map(
        functools.partial(per_device, near_route=near_route, far_route=far_route),
        mesh=mesh,
        in_specs=(P(("grp", "pair"), None), P(("grp", "pair")), P(("grp", "pair"))),
        out_specs=P(("grp", "pair")),
        check_vma=False,
    )
```

time: 64.4 us -> 52.2 us (0.81)
  Pallas kernels: 20.4 us -> 13.1 us
  local copies, waits for them, and re-layouts: 2.27 us -> 0.01 us
  waiting for transfers between devices: 14.7 us -> 12.9 us
    ppermute x1, waiting for transfers between devices: 9.88 us -> 0.96 us  [per_device(): far = [lax.ppermute(own[0], AXES, far_route)]]
    pallas_call x7 -> x8, Pallas kernels: 20.4 us -> 13.1 us  [the longest x5 9.05 us: products(): pl.pallas_call(functools.partial(products_kernel, plan), in_specs=[whole]...]
    ppermute x2, starting transfers between devices: 12.9 us -> 7.05 us  [per_device(): far.append(lax.ppermute(own[-1], AXES, far_route))]
    ppermute x1, starting transfers between devices: 2.04 us -> 7.76 us  [per_device(): far = [lax.ppermute(own[0], AXES, far_route)]]
    ppermute x2, waiting for transfers between devices: 0.01 us -> 3.9 us  [per_device(): near.append(lax.ppermute(own[-1], AXES, near_route))]
    unnamed x10 -> x0, local copies, waits for them, and re-layouts: 2.27 us -> none
    ppermute x1, waiting for transfers between devices: 0.01 us -> 2.01 us  [per_device(): near = [lax.ppermute(own[0], AXES, near_route)]]
    ppermute x2, waiting for transfers between devices: 0.01 us -> 1.25 us  [per_device(): far.append(lax.ppermute(own[-1], AXES, far_route))]
  transfers between devices with their start and end apart: 8 -> 8, of which waited for: 3 -> 7; matrix products, arithmetic and copies ran while one was open for 0% -> 0% of each run, Pallas kernels for 23% -> 19%
where the time goes in v2:
time: 52.2 us; the launch traced here: 51.8 us
  starting transfers between devices  24.5 us (47%)
  Pallas kernels  13.1 us (25%)
  waiting for transfers between devices  12.9 us (25%)
  between operations  0.76 us (1%)
  other arithmetic  0.6 us (1%)
    pallas_call x5, Pallas kernels, products(): pl.pallas_call(functools.partial(products_kernel, plan), in_specs=[whole]...  9.05 us
    ppermute x1, starting transfers between devices, per_device(): far = [lax.ppermute(own[0], AXES, far_route)]  7.76 us
    ppermute x2, starting transfers between devices, per_device(): far.append(lax.ppermute(own[-1], AXES, far_route))  7.05 us
    pallas_call x3, Pallas kernels, normalize(): pl.pallas_call(kernel, in_specs=[in_hbm, pl.BlockSpec(memory_space=pltpu....  4.07 us
    ppermute x2, waiting for transfers between devices, per_device(): near.append(lax.ppermute(own[-1], AXES, near_route))  3.9 us
    ppermute x2, starting transfers between devices, per_device(): near.append(lax.ppermute(own[-1], AXES, near_route))  3.83 us
    ppermute x1, waiting for transfers between devices, per_device(): from_far = lax.ppermute(far_best, AXES, far_route)  3.14 us
    ppermute x1, waiting for transfers between devices, per_device(): near = [lax.ppermute(own[0], AXES, near_route)]  2.01 us
  transfers between devices with their start and end apart: 8, of which 7 were waited for; matrix products, arithmetic and copies ran while one was open for 0% of the time, Pallas kernels for 19%

profile of v2, /device:TPU:6, one launch (start us, length us, event | category | flops | bytes accessed | tf_op | source)
XLA Modules:
  0.0 51.8 jit_solution(1928081027087784484)
XLA Ops:
  0.7 1.5 %normalize.3.refs_3_ = bf16[784,768]{1,0:T(8,128)(2,1)S(1)} custom-call(bf16[1536,768]{1,0:T(8,128)(2,1)} %refs_0_.3, s32[1]{0:T(128)S(6)} %copy.4.refs_1_, s32[12,128]{1,0:T(8,128)} %bitcast.7), custom_call_target="tpu_custom_call" | custom-call | flops 2359296 | bytes 2359296 | tf_op jit(solution)/shard_map/normalize/pallas_call | solution.py:76
  2.2 7.8 %collective-permute-start = (bf16[784,768]{1,0:T(8,128)(2,1)S(1)}, bf16[784,768]{1,0:T(8,128)(2,1)S(1)}, u32[]{:S(2)}, u32[]{:S(2)}) collective-permute-start(bf16[784,768]{1,0:T(8,128)(2,1)S(1)} %normalize.3.refs_3_), channel_id=1, source_target_pairs={{0,12},{1,13},{2,14},{3,15},{4,52},{5,53},{6,54},{7,55},{8,56},{9,... | collective-permute-start | bytes 3612680 | tf_op jit(solution)/shard_map/ppermute | solution.py:185
  10.0 1.9 %collective-permute-start.1 = (bf16[784,768]{1,0:T(8,128)(2,1)S(1)}, bf16[784,768]{1,0:T(8,128)(2,1)S(1)}, u32[]{:S(2)}, u32[]{:S(2)}) collective-permute-start(bf16[784,768]{1,0:T(8,128)(2,1)S(1)} %normalize.3.refs_3_), channel_id=1, source_target_pairs={{0,16},{1,17},{2,18},{3,19},{4,0},{5,1},{6,2},{7,3},{8,12},{9,13},... | collective-permute-start | bytes 3612680 | tf_op jit(solution)/shard_map/ppermute | solution.py:186
  11.9 1.3 %normalize.4.refs_4_ = bf16[512,768]{1,0:T(8,128)(2,1)S(1)} custom-call(bf16[1536,768]{1,0:T(8,128)(2,1)} %refs_0_.3), custom_call_target="tpu_custom_call" | custom-call | flops 1572864 | bytes 1572864 | tf_op jit(solution)/shard_map/normalize/pallas_call | solution.py:76
  13.3 1.9 %collective-permute-start.2 = (bf16[512,768]{1,0:T(8,128)(2,1)S(1)}, bf16[512,768]{1,0:T(8,128)(2,1)S(1)}, u32[]{:S(2)}, u32[]{:S(2)}) collective-permute-start(bf16[512,768]{1,0:T(8,128)(2,1)S(1)} %normalize.4.refs_4_), channel_id=1, source_target_pairs={{0,12},{1,13},{2,14},{3,15},{4,52},{5,53},{6,54},{7,55},{8,56},{9,... | collective-permute-start | bytes 2359304 | tf_op jit(solution)/shard_map/ppermute | solution.py:191
  15.2 1.9 %collective-permute-start.3 = (bf16[512,768]{1,0:T(8,128)(2,1)S(1)}, bf16[512,768]{1,0:T(8,128)(2,1)S(1)}, u32[]{:S(2)}, u32[]{:S(2)}) collective-permute-start(bf16[512,768]{1,0:T(8,128)(2,1)S(1)} %normalize.4.refs_4_), channel_id=1, source_target_pairs={{0,16},{1,17},{2,18},{3,19},{4,0},{5,1},{6,2},{7,3},{8,12},{9,13},... | collective-permute-start | bytes 2359304 | tf_op jit(solution)/shard_map/ppermute | solution.py:192
  17.1 1.2 %normalize.5.refs_5_ = bf16[256,768]{1,0:T(8,128)(2,1)S(1)} custom-call(bf16[1536,768]{1,0:T(8,128)(2,1)} %refs_0_.3), custom_call_target="tpu_custom_call" | custom-call | flops 786432 | bytes 786432 | tf_op jit(solution)/shard_map/normalize/pallas_call | solution.py:76
  18.3 5.1 %collective-permute-start.4 = (bf16[256,768]{1,0:T(8,128)(2,1)S(1)}, bf16[256,768]{1,0:T(8,128)(2,1)S(1)}, u32[]{:S(2)}, u32[]{:S(2)}) collective-permute-start(bf16[256,768]{1,0:T(8,128)(2,1)S(1)} %normalize.5.refs_5_), channel_id=1, source_target_pairs={{0,12},{1,13},{2,14},{3,15},{4,52},{5,53},{6,54},{7,55},{8,56},{9,... | collective-permute-start | bytes 1179656 | tf_op jit(solution)/shard_map/ppermute | solution.py:191
  23.4 1.0 %collective-permute-done.refs_6_.refs_4_.refs_5_ = bf16[784,768]{1,0:T(8,128)(2,1)S(1)} collective-permute-done((bf16[784,768]{1,0:T(8,128)(2,1)S(1)}, bf16[784,768]{1,0:T(8,128)(2,1)S(1)}, u32[]{:S(2)}, u32[]{:S(2)}) %collective-permute-start) | collective-permute-done | bytes 1204256 | tf_op jit(solution)/shard_map/ppermute | solution.py:185
  24.4 1.9 %collective-permute-start.5 = (bf16[256,768]{1,0:T(8,128)(2,1)S(1)}, bf16[256,768]{1,0:T(8,128)(2,1)S(1)}, u32[]{:S(2)}, u32[]{:S(2)}) collective-permute-start(bf16[256,768]{1,0:T(8,128)(2,1)S(1)} %normalize.5.refs_5_), channel_id=1, source_target_pairs={{0,16},{1,17},{2,18},{3,19},{4,0},{5,1},{6,2},{7,3},{8,12},{9,13},... | collective-permute-start | bytes 1179656 | tf_op jit(solution)/shard_map/ppermute | solution.py:192
  26.3 2.0 %collective-permute-done.1.refs_7_.refs_3_.refs_9_.refs_10_ = bf16[784,768]{1,0:T(8,128)(2,1)S(1)} collective-permute-done((bf16[784,768]{1,0:T(8,128)(2,1)S(1)}, bf16[784,768]{1,0:T(8,128)(2,1)S(1)}, u32[]{:S(2)}, u32[]{:S(2)}) %collective-permute-start.1) | collective-permute-done | bytes 1204256 | tf_op jit(solution)/shard_map/ppermute | solution.py:186
  28.3 3.2 %products.5 = (f32[12,128]{1,0:T(8,128)S(1)}, f32[12,128]{1,0:T(8,128)S(1)}, f32[12,128]{1,0:T(8,128)S(1)}) custom-call(f32[12,128]{1,0:T(8,128)S(1)} %broadcast_in_dim.3.refs_0_.refs_1_.refs_2_, f32[12,128]{1,0:T(8,128)S(1)} %broadcast_in_dim.3.refs_0_.refs_1_.refs_2_, f32[12,128]{1,0:T(8,128)S(1)} %broadcast_in_dim.3.refs_0_.refs_1_.refs_2_, ...), custom_call_target="tpu_custom_call" | custom-call | flops 2717908992 | bytes 3538944 | tf_op jit(solution)/shard_map/products/pallas_call | solution.py:163
  31.6 1.3 %collective-permute-done.2.refs_2_.refs_7_ = bf16[512,768]{1,0:T(8,128)(2,1)S(1)} collective-permute-done((bf16[512,768]{1,0:T(8,128)(2,1)S(1)}, bf16[512,768]{1,0:T(8,128)(2,1)S(1)}, u32[]{:S(2)}, u32[]{:S(2)}) %collective-permute-start.2) | collective-permute-done | bytes 786464 | tf_op jit(solution)/shard_map/ppermute | solution.py:191
  32.8 0.9 %products.6 = (f32[12,128]{1,0:T(8,128)S(1)}, f32[12,128]{1,0:T(8,128)S(1)}) custom-call(f32[12,128]{1,0:T(8,128)S(1)} %get-tuple-element.27.refs_0_, f32[12,128]{1,0:T(8,128)S(1)} %get-tuple-element.28.refs_1_, bf16[512,768]{1,0:T(8,128)(2,1)S(1)} %collective-permute-done.2.refs_2_.refs_7_, ...), custom_call_target="tpu_custom_call" | custom-call | flops 603979776 | bytes 786432 | tf_op jit(solution)/shard_map/products/pallas_call | solution.py:163
  33.7 3.0 %collective-permute-done.3.refs_8_.refs_4_ = bf16[512,768]{1,0:T(8,128)(2,1)S(1)} collective-permute-done((bf16[512,768]{1,0:T(8,128)(2,1)S(1)}, bf16[512,768]{1,0:T(8,128)(2,1)S(1)}, u32[]{:S(2)}, u32[]{:S(2)}) %collective-permute-start.3) | collective-permute-done | bytes 786464 | tf_op jit(solution)/shard_map/ppermute | solution.py:192
  36.8 2.5 %products.7 = (f32[12,128]{1,0:T(8,128)S(1)}, f32[12,128]{1,0:T(8,128)S(1)}, f32[12,128]{1,0:T(8,128)S(1)}) custom-call(f32[12,128]{1,0:T(8,128)S(1)} %get-tuple-element.26.refs_0_, f32[12,128]{1,0:T(8,128)S(1)} %get-tuple-element.29.refs_1_, f32[12,128]{1,0:T(8,128)S(1)} %get-tuple-element.30.refs_2_, bf16[784,768]{1,0:T(8,128)(2,1)S(1)} %normalize.3.refs_3_, ...), custom_call_target="tpu_custom_call" | custom-call | flops 2214592512 | bytes 2883584 | tf_op jit(solution)/shard_map/products/pallas_call | solution.py:163
  39.3 0.0 collective-permute-done.4.refs_2_.refs_8_
  39.3 0.8 %products.8 = (f32[12,128]{1,0:T(8,128)S(1)}, f32[12,128]{1,0:T(8,128)S(1)}) custom-call(f32[12,128]{1,0:T(8,128)S(1)} %get-tuple-element.32.refs_0_, f32[12,128]{1,0:T(8,128)S(1)} %get-tuple-element.33.refs_1_, bf16[256,768]{1,0:T(8,128)(2,1)S(1)} %collective-permute-done.4.refs_2_.refs_8_, ...), custom_call_target="tpu_custom_call" | custom-call | flops 503316480 | bytes 655360 | tf_op jit(solution)/shard_map/products/pallas_call | solution.py:163
  40.1 0.9 %collective-permute-done.5.refs_9_ = bf16[256,768]{1,0:T(8,128)(2,1)S(1)} collective-permute-done((bf16[256,768]{1,0:T(8,128)(2,1)S(1)}, bf16[256,768]{1,0:T(8,128)(2,1)S(1)}, u32[]{:S(2)}, u32[]{:S(2)}) %collective-permute-start.5) | collective-permute-done | bytes 393248 | tf_op jit(solution)/shard_map/ppermute | solution.py:192
  41.0 1.6 %products.9 = (f32[12,128]{1,0:T(8,128)S(1)}, f32[12,128]{1,0:T(8,128)S(1)}, f32[12,128]{1,0:T(8,128)S(1)}) custom-call(f32[12,128]{1,0:T(8,128)S(1)} %get-tuple-element.31.refs_0_, f32[12,128]{1,0:T(8,128)S(1)} %get-tuple-element.34.refs_1_, f32[12,128]{1,0:T(8,128)S(1)} %get-tuple-element.35.refs_2_, bf16[784,768]{1,0:T(8,128)(2,1)S(1)} %normalize.3.refs_3_, ...), custom_call_target="tpu_custom_call" | custom-call | flops 1207959552 | bytes 1572864 | tf_op jit(solution)/shard_map/products/pallas_call | solution.py:163
  42.6 1.9 %collective-permute-start.6 = (f32[1536]{0:T(1024)S(1)}, f32[1536]{0:T(1024)S(1)}, u32[]{:S(2)}, u32[]{:S(2)}) collective-permute-start(f32[1536]{0:T(1024)S(1)} %bitcast.6), channel_id=1, source_target_pairs={{16,0},{17,1},{18,2},{19,3},{0,4},{1,5},{2,6},{3,7},{12,8},{13,9},... | collective-permute-start | bytes 18440 | tf_op jit(solution)/shard_map/ppermute | solution.py:205
  44.5 2.0 %collective-permute-start.7 = (f32[1536]{0:T(1024)S(1)}, f32[1536]{0:T(1024)S(1)}, u32[]{:S(2)}, u32[]{:S(2)}) collective-permute-start(f32[1536]{0:T(1024)S(1)} %bitcast.5), channel_id=1, source_target_pairs={{0,12},{1,13},{2,14},{3,15},{4,52},{5,53},{6,54},{7,55},{8,56},{9,... | collective-permute-start | bytes 18440 | tf_op jit(solution)/shard_map/ppermute | solution.py:206
  46.5 1.6 %collective-permute-done.6 = f32[1536]{0:T(1024)S(1)} collective-permute-done((f32[1536]{0:T(1024)S(1)}, f32[1536]{0:T(1024)S(1)}, u32[]{:S(2)}, u32[]{:S(2)}) %collective-permute-start.6) | collective-permute-done | bytes 6176 | tf_op jit(solution)/shard_map/ppermute | solution.py:205
  48.1 3.1 %collective-permute-done.7 = f32[1536]{0:T(1024)S(1)} collective-permute-done((f32[1536]{0:T(1024)S(1)}, f32[1536]{0:T(1024)S(1)}, u32[]{:S(2)}, u32[]{:S(2)}) %collective-permute-start.7) | collective-permute-done | bytes 6176 | tf_op jit(solution)/shard_map/ppermute | solution.py:206
  51.2 0.6 %bitcast_maximum_fusion = f32[1536]{0:T(1024)} fusion(f32[12,128]{1,0:T(8,128)S(1)} %get-tuple-element.36, f32[1536]{0:T(1024)S(1)} %collective-permute-done.6, f32[1536]{0:T(1024)S(1)} %collective-permute-done.7), kind=kLoop, calls=%fused_computation | loop fusion | flops 3072 | bytes 24576 | tf_op jit(solution)/shard_map/max | solution.py:207
  (1 shorter events, 0.0 us)
Async XLA Ops:
  2.2 22.2 %collective-permute-start = (bf16[784,768]{1,0:T(8,128)(2,1)S(1)}, bf16[784,768]{1,0:T(8,128)(2,1)S(1)}, u32[]{:S(2)}, u32[]{:S(2)}) collective-permute-start(bf16[784,768]{1,0:T(8,128)(2,1)S(1)} %normalize.3.refs_3_), channel_id=1, source_target_pairs={{0,12},{1,13},{2,14},{3,15},{4,52},{5,53},{6,54},{7,55},{8,56},{9,... | collective-permute-start | bytes 3612680 | tf_op jit(solution)/shard_map/ppermute | solution.py:185
  10.0 18.4 %collective-permute-start.1 = (bf16[784,768]{1,0:T(8,128)(2,1)S(1)}, bf16[784,768]{1,0:T(8,128)(2,1)S(1)}, u32[]{:S(2)}, u32[]{:S(2)}) collective-permute-start(bf16[784,768]{1,0:T(8,128)(2,1)S(1)} %normalize.3.refs_3_), channel_id=1, source_target_pairs={{0,16},{1,17},{2,18},{3,19},{4,0},{5,1},{6,2},{7,3},{8,12},{9,13},... | collective-permute-start | bytes 3612680 | tf_op jit(solution)/shard_map/ppermute | solution.py:186
  13.3 19.6 %collective-permute-start.2 = (bf16[512,768]{1,0:T(8,128)(2,1)S(1)}, bf16[512,768]{1,0:T(8,128)(2,1)S(1)}, u32[]{:S(2)}, u32[]{:S(2)}) collective-permute-start(bf16[512,768]{1,0:T(8,128)(2,1)S(1)} %normalize.4.refs_4_), channel_id=1, source_target_pairs={{0,12},{1,13},{2,14},{3,15},{4,52},{5,53},{6,54},{7,55},{8,56},{9,... | collective-permute-start | bytes 2359304 | tf_op jit(solution)/shard_map/ppermute | solution.py:191
  15.2 21.6 %collective-permute-start.3 = (bf16[512,768]{1,0:T(8,128)(2,1)S(1)}, bf16[512,768]{1,0:T(8,128)(2,1)S(1)}, u32[]{:S(2)}, u32[]{:S(2)}) collective-permute-start(bf16[512,768]{1,0:T(8,128)(2,1)S(1)} %normalize.4.refs_4_), channel_id=1, source_target_pairs={{0,16},{1,17},{2,18},{3,19},{4,0},{5,1},{6,2},{7,3},{8,12},{9,13},... | collective-permute-start | bytes 2359304 | tf_op jit(solution)/shard_map/ppermute | solution.py:192
  18.3 21.0 %collective-permute-start.4 = (bf16[256,768]{1,0:T(8,128)(2,1)S(1)}, bf16[256,768]{1,0:T(8,128)(2,1)S(1)}, u32[]{:S(2)}, u32[]{:S(2)}) collective-permute-start(bf16[256,768]{1,0:T(8,128)(2,1)S(1)} %normalize.5.refs_5_), channel_id=1, source_target_pairs={{0,12},{1,13},{2,14},{3,15},{4,52},{5,53},{6,54},{7,55},{8,56},{9,... | collective-permute-start | bytes 1179656 | tf_op jit(solution)/shard_map/ppermute | solution.py:191
  24.4 16.6 %collective-permute-start.5 = (bf16[256,768]{1,0:T(8,128)(2,1)S(1)}, bf16[256,768]{1,0:T(8,128)(2,1)S(1)}, u32[]{:S(2)}, u32[]{:S(2)}) collective-permute-start(bf16[256,768]{1,0:T(8,128)(2,1)S(1)} %normalize.5.refs_5_), channel_id=1, source_target_pairs={{0,16},{1,17},{2,18},{3,19},{4,0},{5,1},{6,2},{7,3},{8,12},{9,13},... | collective-permute-start | bytes 1179656 | tf_op jit(solution)/shard_map/ppermute | solution.py:192
  42.6 5.5 %collective-permute-start.6 = (f32[1536]{0:T(1024)S(1)}, f32[1536]{0:T(1024)S(1)}, u32[]{:S(2)}, u32[]{:S(2)}) collective-permute-start(f32[1536]{0:T(1024)S(1)} %bitcast.6), channel_id=1, source_target_pairs={{16,0},{17,1},{18,2},{19,3},{0,4},{1,5},{2,6},{3,7},{12,8},{13,9},... | collective-permute-start | bytes 18440 | tf_op jit(solution)/shard_map/ppermute | solution.py:205
  44.5 6.8 %collective-permute-start.7 = (f32[1536]{0:T(1024)S(1)}, f32[1536]{0:T(1024)S(1)}, u32[]{:S(2)}, u32[]{:S(2)}) collective-permute-start(f32[1536]{0:T(1024)S(1)} %bitcast.5), channel_id=1, source_target_pairs={{0,12},{1,13},{2,14},{3,15},{4,52},{5,53},{6,54},{7,55},{8,56},{9,... | collective-permute-start | bytes 18440 | tf_op jit(solution)/shard_map/ppermute | solution.py:206

commit v3 on v2

--- a/solution.py
+++ b/solution.py
@@ -195,12 +195,11 @@
     last = len(sizes) - 1
     every = range(len(sizes))
     fold = functools.partial(products, own=own, far=far, near=near, sizes=sizes)
-    state = fold(state, want={(0, r, 0) for r in every} | {(1, 0, 0)})
-    for c in range(1, last):
-        state = fold(state, want={(1, c, k) for k in range(c)})
-        state = fold(state, want={(0, r, c) for r in every} | {(1, r, c) for r in range(c + 1)})
-    state = fold(state, want={(1, last, k) for k in range(last)})
-    state = fold(state, want={(0, r, last) for r in every} | {(1, r, last) for r in every})
+    state = fold(state, want={(0, r, 0) for r in every})
+    state = fold(state, want={(1, 0, 0)})
+    for c in range(1, len(sizes)):
+        state = fold(state, want={(0, r, c) for r in every} | {(1, r, c) for r in range(c)})
+        state = fold(state, want={(1, c, k) for k in range(c + 1)})
     kept, far_best, near_best = [s.reshape(rows) for s in state]
     from_near = lax.ppermute(near_best, AXES, back_route)
     from_far = lax.ppermute(far_best, AXES, far_route)

time: 52.2 us -> 52.8 us (1.011)
  the two profiles are of different devices: /device:TPU:6 before, /device:TPU:2 now
where the time goes in v3:
time: 52.8 us; the launch traced here: 52.4 us
  starting transfers between devices  24.5 us (46%)
  Pallas kernels  13.3 us (25%)
  waiting for transfers between devices  13.3 us (25%)
  between operations  0.78 us (1%)
  other arithmetic  0.6 us (1%)
    pallas_call x6, Pallas kernels, products(): pl.pallas_call(functools.partial(products_kernel, plan), in_specs=[whole]...  9.2 us
    ppermute x1, starting transfers between devices, per_device(): near = [lax.ppermute(own[0], AXES, near_route)]  7.82 us
    ppermute x2, starting transfers between devices, per_device(): far.append(lax.ppermute(own[-1], AXES, far_route))  7.04 us
    ppermute x2, waiting for transfers between devices, per_device(): far.append(lax.ppermute(own[-1], AXES, far_route))  4.93 us
    pallas_call x3, Pallas kernels, normalize(): pl.pallas_call(kernel, in_specs=[in_hbm, pl.BlockSpec(memory_space=pltpu....  4.07 us
    ppermute x2, starting transfers between devices, per_device(): near.append(lax.ppermute(own[-1], AXES, near_route))  3.84 us
    ppermute x1, waiting for transfers between devices, per_device(): from_far = lax.ppermute(far_best, AXES, far_route)  3.14 us
    ppermute x1, starting transfers between devices, per_device(): far = [lax.ppermute(own[0], AXES, far_route)]  1.92 us
  transfers between devices with their start and end apart: 8, of which 7 were waited for; matrix products, arithmetic and copies ran while one was open for 0% of the time, Pallas kernels for 21%

profile of v3, /device:TPU:2, one launch (start us, length us, event | category | flops | bytes accessed | tf_op | source)
XLA Modules:
  0.0 52.4 jit_solution(5015336155101487224)
XLA Ops:
  0.7 1.5 %normalize.3.refs_2_.refs_3_ = bf16[784,768]{1,0:T(8,128)(2,1)S(1)} custom-call(bf16[1536,768]{1,0:T(8,128)(2,1)} %refs_0_.3, s32[1]{0:T(128)S(6)} %copy.4.refs_1_, s32[12,128]{1,0:T(8,128)} %bitcast.7), custom_call_target="tpu_custom_call" | custom-call | flops 2359296 | bytes 2359296 | tf_op jit(solution)/shard_map/normalize/pallas_call | solution.py:76
  2.2 7.8 %collective-permute-start = (bf16[784,768]{1,0:T(8,128)(2,1)S(1)}, bf16[784,768]{1,0:T(8,128)(2,1)S(1)}, u32[]{:S(2)}, u32[]{:S(2)}) collective-permute-start(bf16[784,768]{1,0:T(8,128)(2,1)S(1)} %normalize.3.refs_2_.refs_3_), channel_id=1, source_target_pairs={{0,16},{1,17},{2,18},{3,19},{4,0},{5,1},{6,2},{7,3},{8,12},{9,13},... | collective-permute-start | bytes 3612680 | tf_op jit(solution)/shard_map/ppermute | solution.py:186
  10.0 1.9 %collective-permute-start.1 = (bf16[784,768]{1,0:T(8,128)(2,1)S(1)}, bf16[784,768]{1,0:T(8,128)(2,1)S(1)}, u32[]{:S(2)}, u32[]{:S(2)}) collective-permute-start(bf16[784,768]{1,0:T(8,128)(2,1)S(1)} %normalize.3.refs_2_.refs_3_), channel_id=1, source_target_pairs={{0,12},{1,13},{2,14},{3,15},{4,52},{5,53},{6,54},{7,55},{8,56},{9,... | collective-permute-start | bytes 3612680 | tf_op jit(solution)/shard_map/ppermute | solution.py:185
  12.0 1.3 %normalize.4.refs_3_.refs_4_ = bf16[512,768]{1,0:T(8,128)(2,1)S(1)} custom-call(bf16[1536,768]{1,0:T(8,128)(2,1)} %refs_0_.3), custom_call_target="tpu_custom_call" | custom-call | flops 1572864 | bytes 1572864 | tf_op jit(solution)/shard_map/normalize/pallas_call | solution.py:76
  13.3 1.9 %collective-permute-start.2 = (bf16[512,768]{1,0:T(8,128)(2,1)S(1)}, bf16[512,768]{1,0:T(8,128)(2,1)S(1)}, u32[]{:S(2)}, u32[]{:S(2)}) collective-permute-start(bf16[512,768]{1,0:T(8,128)(2,1)S(1)} %normalize.4.refs_3_.refs_4_), channel_id=1, source_target_pairs={{0,16},{1,17},{2,18},{3,19},{4,0},{5,1},{6,2},{7,3},{8,12},{9,13},... | collective-permute-start | bytes 2359304 | tf_op jit(solution)/shard_map/ppermute | solution.py:192
  15.2 5.1 %collective-permute-start.3 = (bf16[512,768]{1,0:T(8,128)(2,1)S(1)}, bf16[512,768]{1,0:T(8,128)(2,1)S(1)}, u32[]{:S(2)}, u32[]{:S(2)}) collective-permute-start(bf16[512,768]{1,0:T(8,128)(2,1)S(1)} %normalize.4.refs_3_.refs_4_), channel_id=1, source_target_pairs={{0,12},{1,13},{2,14},{3,15},{4,52},{5,53},{6,54},{7,55},{8,56},{9,... | collective-permute-start | bytes 2359304 | tf_op jit(solution)/shard_map/ppermute | solution.py:191
  20.4 1.2 %normalize.5.refs_4_.refs_5_ = bf16[256,768]{1,0:T(8,128)(2,1)S(1)} custom-call(bf16[1536,768]{1,0:T(8,128)(2,1)} %refs_0_.3), custom_call_target="tpu_custom_call" | custom-call | flops 786432 | bytes 786432 | tf_op jit(solution)/shard_map/normalize/pallas_call | solution.py:76
  21.6 1.9 %collective-permute-start.4 = (bf16[256,768]{1,0:T(8,128)(2,1)S(1)}, bf16[256,768]{1,0:T(8,128)(2,1)S(1)}, u32[]{:S(2)}, u32[]{:S(2)}) collective-permute-start(bf16[256,768]{1,0:T(8,128)(2,1)S(1)} %normalize.5.refs_4_.refs_5_), channel_id=1, source_target_pairs={{0,16},{1,17},{2,18},{3,19},{4,0},{5,1},{6,2},{7,3},{8,12},{9,13},... | collective-permute-start | bytes 1179656 | tf_op jit(solution)/shard_map/ppermute | solution.py:192
  23.5 0.5 collective-permute-done.refs_5_.refs_3_.refs_8_.refs_9_
  24.0 1.9 %collective-permute-start.5 = (bf16[256,768]{1,0:T(8,128)(2,1)S(1)}, bf16[256,768]{1,0:T(8,128)(2,1)S(1)}, u32[]{:S(2)}, u32[]{:S(2)}) collective-permute-start(bf16[256,768]{1,0:T(8,128)(2,1)S(1)} %normalize.5.refs_4_.refs_5_), channel_id=1, source_target_pairs={{0,12},{1,13},{2,14},{3,15},{4,52},{5,53},{6,54},{7,55},{8,56},{9,... | collective-permute-start | bytes 1179656 | tf_op jit(solution)/shard_map/ppermute | solution.py:191
  25.9 2.2 %products.6 = (f32[12,128]{1,0:T(8,128)S(1)}, f32[12,128]{1,0:T(8,128)S(1)}) custom-call(f32[12,128]{1,0:T(8,128)S(1)} %broadcast_in_dim.3.refs_0_.refs_1_, f32[12,128]{1,0:T(8,128)S(1)} %broadcast_in_dim.3.refs_0_.refs_1_, bf16[784,768]{1,0:T(8,128)(2,1)S(1)} %normalize.3.refs_2_.refs_3_, bf16[512,768]{1,0:T(8,128)(2,1)S(1)} %normalize.4.refs_3_.refs_4_, ...), custom_call_target="tpu_custom_call" | custom-call | flops 1811939328 | bytes 2359296 | tf_op jit(solution)/shard_map/products/pallas_call | solution.py:163
  28.1 1.5 %collective-permute-done.1.refs_2_.refs_6_.refs_5_ = bf16[784,768]{1,0:T(8,128)(2,1)S(1)} collective-permute-done((bf16[784,768]{1,0:T(8,128)(2,1)S(1)}, bf16[784,768]{1,0:T(8,128)(2,1)S(1)}, u32[]{:S(2)}, u32[]{:S(2)}) %collective-permute-start.1) | collective-permute-done | bytes 1204256 | tf_op jit(solution)/shard_map/ppermute | solution.py:185
  29.6 1.3 %products.7 = (f32[12,128]{1,0:T(8,128)S(1)}, f32[12,128]{1,0:T(8,128)S(1)}) custom-call(f32[12,128]{1,0:T(8,128)S(1)} %broadcast_in_dim.3.refs_0_.refs_1_, f32[12,128]{1,0:T(8,128)S(1)} %get-tuple-element.28.refs_1_, bf16[784,768]{1,0:T(8,128)(2,1)S(1)} %collective-permute-done.1.refs_2_.refs_6_.refs_5_, ...), custom_call_target="tpu_custom_call" | custom-call | flops 905969664 | bytes 1179648 | tf_op jit(solution)/shard_map/products/pallas_call | solution.py:163
  30.9 1.6 %collective-permute-done.2.refs_7_.refs_4_ = bf16[512,768]{1,0:T(8,128)(2,1)S(1)} collective-permute-done((bf16[512,768]{1,0:T(8,128)(2,1)S(1)}, bf16[512,768]{1,0:T(8,128)(2,1)S(1)}, u32[]{:S(2)}, u32[]{:S(2)}) %collective-permute-start.2) | collective-permute-done | bytes 786464 | tf_op jit(solution)/shard_map/ppermute | solution.py:192
  32.4 2.1 %products.8 = (f32[12,128]{1,0:T(8,128)S(1)}, f32[12,128]{1,0:T(8,128)S(1)}, f32[12,128]{1,0:T(8,128)S(1)}) custom-call(f32[12,128]{1,0:T(8,128)S(1)} %get-tuple-element.27.refs_0_, f32[12,128]{1,0:T(8,128)S(1)} %get-tuple-element.29.refs_1_, f32[12,128]{1,0:T(8,128)S(1)} %get-tuple-element.30.refs_2_, bf16[784,768]{1,0:T(8,128)(2,1)S(1)} %normalize.3.refs_2_.refs_3_, ...), custom_call_target="tpu_custom_call" | custom-call | flops 1811939328 | bytes 2359296 | tf_op jit(solution)/shard_map/products/pallas_call | solution.py:163
  34.5 3.5 %collective-permute-done.3.refs_2_.refs_7_ = bf16[512,768]{1,0:T(8,128)(2,1)S(1)} collective-permute-done((bf16[512,768]{1,0:T(8,128)(2,1)S(1)}, bf16[512,768]{1,0:T(8,128)(2,1)S(1)}, u32[]{:S(2)}, u32[]{:S(2)}) %collective-permute-start.3) | collective-permute-done | bytes 786464 | tf_op jit(solution)/shard_map/ppermute | solution.py:191
  38.0 1.3 %products.9 = (f32[12,128]{1,0:T(8,128)S(1)}, f32[12,128]{1,0:T(8,128)S(1)}) custom-call(f32[12,128]{1,0:T(8,128)S(1)} %get-tuple-element.32.refs_0_, f32[12,128]{1,0:T(8,128)S(1)} %get-tuple-element.33.refs_1_, bf16[512,768]{1,0:T(8,128)(2,1)S(1)} %collective-permute-done.3.refs_2_.refs_7_, ...), custom_call_target="tpu_custom_call" | custom-call | flops 1006632960 | bytes 1310720 | tf_op jit(solution)/shard_map/products/pallas_call | solution.py:163
  39.3 0.0 collective-permute-done.4.refs_8_.refs_5_
  39.4 1.4 %products.10 = (f32[12,128]{1,0:T(8,128)S(1)}, f32[12,128]{1,0:T(8,128)S(1)}, f32[12,128]{1,0:T(8,128)S(1)}) custom-call(f32[12,128]{1,0:T(8,128)S(1)} %get-tuple-element.31.refs_0_, f32[12,128]{1,0:T(8,128)S(1)} %get-tuple-element.34.refs_1_, f32[12,128]{1,0:T(8,128)S(1)} %get-tuple-element.35.refs_2_, bf16[784,768]{1,0:T(8,128)(2,1)S(1)} %normalize.3.refs_2_.refs_3_, ...), custom_call_target="tpu_custom_call" | custom-call | flops 1107296256 | bytes 1441792 | tf_op jit(solution)/shard_map/products/pallas_call | solution.py:163
  40.8 1.4 %collective-permute-done.5.refs_2_ = bf16[256,768]{1,0:T(8,128)(2,1)S(1)} collective-permute-done((bf16[256,768]{1,0:T(8,128)(2,1)S(1)}, bf16[256,768]{1,0:T(8,128)(2,1)S(1)}, u32[]{:S(2)}, u32[]{:S(2)}) %collective-permute-start.5) | collective-permute-done | bytes 393248 | tf_op jit(solution)/shard_map/ppermute | solution.py:191
  42.2 0.9 %products.11 = (f32[12,128]{1,0:T(8,128)S(1)}, f32[12,128]{1,0:T(8,128)S(1)}) custom-call(f32[12,128]{1,0:T(8,128)S(1)} %get-tuple-element.37.refs_0_, f32[12,128]{1,0:T(8,128)S(1)} %get-tuple-element.38.refs_1_, bf16[256,768]{1,0:T(8,128)(2,1)S(1)} %collective-permute-done.5.refs_2_, ...), custom_call_target="tpu_custom_call" | custom-call | flops 603979776 | bytes 786432 | tf_op jit(solution)/shard_map/products/pallas_call | solution.py:163
  43.1 1.9 %collective-permute-start.6 = (f32[1536]{0:T(1024)S(1)}, f32[1536]{0:T(1024)S(1)}, u32[]{:S(2)}, u32[]{:S(2)}) collective-permute-start(f32[1536]{0:T(1024)S(1)} %bitcast.6), channel_id=1, source_target_pairs={{16,0},{17,1},{18,2},{19,3},{0,4},{1,5},{2,6},{3,7},{12,8},{13,9},... | collective-permute-start | bytes 18440 | tf_op jit(solution)/shard_map/ppermute | solution.py:204
  45.1 1.9 %collective-permute-start.7 = (f32[1536]{0:T(1024)S(1)}, f32[1536]{0:T(1024)S(1)}, u32[]{:S(2)}, u32[]{:S(2)}) collective-permute-start(f32[1536]{0:T(1024)S(1)} %bitcast.5), channel_id=1, source_target_pairs={{0,12},{1,13},{2,14},{3,15},{4,52},{5,53},{6,54},{7,55},{8,56},{9,... | collective-permute-start | bytes 18440 | tf_op jit(solution)/shard_map/ppermute | solution.py:205
  47.0 1.7 %collective-permute-done.6 = f32[1536]{0:T(1024)S(1)} collective-permute-done((f32[1536]{0:T(1024)S(1)}, f32[1536]{0:T(1024)S(1)}, u32[]{:S(2)}, u32[]{:S(2)}) %collective-permute-start.6) | collective-permute-done | bytes 6176 | tf_op jit(solution)/shard_map/ppermute | solution.py:204
  48.7 3.1 %collective-permute-done.7 = f32[1536]{0:T(1024)S(1)} collective-permute-done((f32[1536]{0:T(1024)S(1)}, f32[1536]{0:T(1024)S(1)}, u32[]{:S(2)}, u32[]{:S(2)}) %collective-permute-start.7) | collective-permute-done | bytes 6176 | tf_op jit(solution)/shard_map/ppermute | solution.py:205
  51.8 0.6 %bitcast_maximum_fusion = f32[1536]{0:T(1024)} fusion(f32[12,128]{1,0:T(8,128)S(1)} %get-tuple-element.36, f32[1536]{0:T(1024)S(1)} %collective-permute-done.6, f32[1536]{0:T(1024)S(1)} %collective-permute-done.7), kind=kLoop, calls=%fused_computation | loop fusion | flops 3072 | bytes 24576 | tf_op jit(solution)/shard_map/max | solution.py:206
  (1 shorter events, 0.0 us)
Async XLA Ops:
  2.2 21.8 %collective-permute-start = (bf16[784,768]{1,0:T(8,128)(2,1)S(1)}, bf16[784,768]{1,0:T(8,128)(2,1)S(1)}, u32[]{:S(2)}, u32[]{:S(2)}) collective-permute-start(bf16[784,768]{1,0:T(8,128)(2,1)S(1)} %normalize.3.refs_2_.refs_3_), channel_id=1, source_target_pairs={{0,16},{1,17},{2,18},{3,19},{4,0},{5,1},{6,2},{7,3},{8,12},{9,13},... | collective-permute-start | bytes 3612680 | tf_op jit(solution)/shard_map/ppermute | solution.py:186
  10.0 19.6 %collective-permute-start.1 = (bf16[784,768]{1,0:T(8,128)(2,1)S(1)}, bf16[784,768]{1,0:T(8,128)(2,1)S(1)}, u32[]{:S(2)}, u32[]{:S(2)}) collective-permute-start(bf16[784,768]{1,0:T(8,128)(2,1)S(1)} %normalize.3.refs_2_.refs_3_), channel_id=1, source_target_pairs={{0,12},{1,13},{2,14},{3,15},{4,52},{5,53},{6,54},{7,55},{8,56},{9,... | collective-permute-start | bytes 3612680 | tf_op jit(solution)/shard_map/ppermute | solution.py:185
  13.3 19.1 %collective-permute-start.2 = (bf16[512,768]{1,0:T(8,128)(2,1)S(1)}, bf16[512,768]{1,0:T(8,128)(2,1)S(1)}, u32[]{:S(2)}, u32[]{:S(2)}) collective-permute-start(bf16[512,768]{1,0:T(8,128)(2,1)S(1)} %normalize.4.refs_3_.refs_4_), channel_id=1, source_target_pairs={{0,16},{1,17},{2,18},{3,19},{4,0},{5,1},{6,2},{7,3},{8,12},{9,13},... | collective-permute-start | bytes 2359304 | tf_op jit(solution)/shard_map/ppermute | solution.py:192
  15.2 22.8 %collective-permute-start.3 = (bf16[512,768]{1,0:T(8,128)(2,1)S(1)}, bf16[512,768]{1,0:T(8,128)(2,1)S(1)}, u32[]{:S(2)}, u32[]{:S(2)}) collective-permute-start(bf16[512,768]{1,0:T(8,128)(2,1)S(1)} %normalize.4.refs_3_.refs_4_), channel_id=1, source_target_pairs={{0,12},{1,13},{2,14},{3,15},{4,52},{5,53},{6,54},{7,55},{8,56},{9,... | collective-permute-start | bytes 2359304 | tf_op jit(solution)/shard_map/ppermute | solution.py:191
  21.6 17.8 %collective-permute-start.4 = (bf16[256,768]{1,0:T(8,128)(2,1)S(1)}, bf16[256,768]{1,0:T(8,128)(2,1)S(1)}, u32[]{:S(2)}, u32[]{:S(2)}) collective-permute-start(bf16[256,768]{1,0:T(8,128)(2,1)S(1)} %normalize.5.refs_4_.refs_5_), channel_id=1, source_target_pairs={{0,16},{1,17},{2,18},{3,19},{4,0},{5,1},{6,2},{7,3},{8,12},{9,13},... | collective-permute-start | bytes 1179656 | tf_op jit(solution)/shard_map/ppermute | solution.py:192
  24.0 18.2 %collective-permute-start.5 = (bf16[256,768]{1,0:T(8,128)(2,1)S(1)}, bf16[256,768]{1,0:T(8,128)(2,1)S(1)}, u32[]{:S(2)}, u32[]{:S(2)}) collective-permute-start(bf16[256,768]{1,0:T(8,128)(2,1)S(1)} %normalize.5.refs_4_.refs_5_), channel_id=1, source_target_pairs={{0,12},{1,13},{2,14},{3,15},{4,52},{5,53},{6,54},{7,55},{8,56},{9,... | collective-permute-start | bytes 1179656 | tf_op jit(solution)/shard_map/ppermute | solution.py:191
  43.1 5.5 %collective-permute-start.6 = (f32[1536]{0:T(1024)S(1)}, f32[1536]{0:T(1024)S(1)}, u32[]{:S(2)}, u32[]{:S(2)}) collective-permute-start(f32[1536]{0:T(1024)S(1)} %bitcast.6), channel_id=1, source_target_pairs={{16,0},{17,1},{18,2},{19,3},{0,4},{1,5},{2,6},{3,7},{12,8},{13,9},... | collective-permute-start | bytes 18440 | tf_op jit(solution)/shard_map/ppermute | solution.py:204
  45.1 6.8 %collective-permute-start.7 = (f32[1536]{0:T(1024)S(1)}, f32[1536]{0:T(1024)S(1)}, u32[]{:S(2)}, u32[]{:S(2)}) collective-permute-start(f32[1536]{0:T(1024)S(1)} %bitcast.5), channel_id=1, source_target_pairs={{0,12},{1,13},{2,14},{3,15},{4,52},{5,53},{6,54},{7,55},{8,56},{9,... | collective-permute-start | bytes 18440 | tf_op jit(solution)/shard_map/ppermute | solution.py:205

commit v4 on v2

--- a/solution.py
+++ b/solution.py
@@ -202,9 +202,9 @@
     state = fold(state, want={(1, last, k) for k in range(last)})
     state = fold(state, want={(0, r, last) for r in every} | {(1, r, last) for r in every})
     kept, far_best, near_best = [s.reshape(rows) for s in state]
+    from_far = lax.ppermute(far_best, AXES, far_route)
     from_near = lax.ppermute(near_best, AXES, back_route)
-    from_far = lax.ppermute(far_best, AXES, far_route)
-    return jnp.maximum(kept, jnp.maximum(from_near, from_far))
+    return jnp.maximum(jnp.maximum(kept, from_near), from_far)
 
 
 def solution(mesh):

time: 52.2 us -> 52.3 us (level)
  the two profiles are of different devices: /device:TPU:6 before, /device:TPU:2 now
where the time goes in v4:
time: 52.3 us; the launch traced here: 51.9 us
  starting transfers between devices  29.2 us (56%)
  Pallas kernels  13.1 us (25%)
  waiting for transfers between devices  8.17 us (16%)
  between operations  0.79 us (2%)
  other arithmetic  0.6 us (1%)
    ppermute x2, starting transfers between devices, per_device(): near.append(lax.ppermute(own[-1], AXES, near_route))  10.8 us
    pallas_call x5, Pallas kernels, products(): pl.pallas_call(functools.partial(products_kernel, plan), in_specs=[whole]...  9.06 us
    ppermute x1, starting transfers between devices, per_device(): far = [lax.ppermute(own[0], AXES, far_route)]  4.92 us
    ppermute x1, starting transfers between devices, per_device(): near = [lax.ppermute(own[0], AXES, near_route)]  4.81 us
    ppermute x1, waiting for transfers between devices, per_device(): from_near = lax.ppermute(near_best, AXES, back_route)  4.4 us
    ppermute x2, starting transfers between devices, per_device(): far.append(lax.ppermute(own[-1], AXES, far_route))  4.22 us
    pallas_call x3, Pallas kernels, normalize(): pl.pallas_call(kernel, in_specs=[in_hbm, pl.BlockSpec(memory_space=pltpu....  4.07 us
    ppermute x1, waiting for transfers between devices, per_device(): from_far = lax.ppermute(far_best, AXES, far_route)  2.31 us
  transfers between devices with their start and end apart: 8, of which 4 were waited for; matrix products, arithmetic and copies ran while one was open for 0% of the time, Pallas kernels for 19%

profile of v4, /device:TPU:2, one launch (start us, length us, event | category | flops | bytes accessed | tf_op | source)
XLA Modules:
  0.0 51.9 jit_solution(6620652635991593749)
XLA Ops:
  0.7 1.5 %normalize.3.refs_3_ = bf16[784,768]{1,0:T(8,128)(2,1)S(1)} custom-call(bf16[1536,768]{1,0:T(8,128)(2,1)} %refs_0_.3, s32[1]{0:T(128)S(6)} %copy.4.refs_1_, s32[12,128]{1,0:T(8,128)} %bitcast.9), custom_call_target="tpu_custom_call" | custom-call | flops 2359296 | bytes 2359296 | tf_op jit(solution)/shard_map/normalize/pallas_call | solution.py:76
  2.2 4.9 %collective-permute-start = (bf16[784,768]{1,0:T(8,128)(2,1)S(1)}, bf16[784,768]{1,0:T(8,128)(2,1)S(1)}, u32[]{:S(2)}, u32[]{:S(2)}) collective-permute-start(bf16[784,768]{1,0:T(8,128)(2,1)S(1)} %normalize.3.refs_3_), channel_id=1, source_target_pairs={{0,12},{1,13},{2,14},{3,15},{4,52},{5,53},{6,54},{7,55},{8,56},{9,... | collective-permute-start | bytes 3612680 | tf_op jit(solution)/shard_map/ppermute | solution.py:185
  7.1 4.8 %collective-permute-start.1 = (bf16[784,768]{1,0:T(8,128)(2,1)S(1)}, bf16[784,768]{1,0:T(8,128)(2,1)S(1)}, u32[]{:S(2)}, u32[]{:S(2)}) collective-permute-start(bf16[784,768]{1,0:T(8,128)(2,1)S(1)} %normalize.3.refs_3_), channel_id=1, source_target_pairs={{0,16},{1,17},{2,18},{3,19},{4,0},{5,1},{6,2},{7,3},{8,12},{9,13},... | collective-permute-start | bytes 3612680 | tf_op jit(solution)/shard_map/ppermute | solution.py:186
  12.0 1.3 %normalize.4.refs_4_ = bf16[512,768]{1,0:T(8,128)(2,1)S(1)} custom-call(bf16[1536,768]{1,0:T(8,128)(2,1)} %refs_0_.3), custom_call_target="tpu_custom_call" | custom-call | flops 1572864 | bytes 1572864 | tf_op jit(solution)/shard_map/normalize/pallas_call | solution.py:76
  13.3 2.3 %collective-permute-start.2 = (bf16[512,768]{1,0:T(8,128)(2,1)S(1)}, bf16[512,768]{1,0:T(8,128)(2,1)S(1)}, u32[]{:S(2)}, u32[]{:S(2)}) collective-permute-start(bf16[512,768]{1,0:T(8,128)(2,1)S(1)} %normalize.4.refs_4_), channel_id=1, source_target_pairs={{0,12},{1,13},{2,14},{3,15},{4,52},{5,53},{6,54},{7,55},{8,56},{9,... | collective-permute-start | bytes 2359304 | tf_op jit(solution)/shard_map/ppermute | solution.py:191
  15.6 4.8 %collective-permute-start.3 = (bf16[512,768]{1,0:T(8,128)(2,1)S(1)}, bf16[512,768]{1,0:T(8,128)(2,1)S(1)}, u32[]{:S(2)}, u32[]{:S(2)}) collective-permute-start(bf16[512,768]{1,0:T(8,128)(2,1)S(1)} %normalize.4.refs_4_), channel_id=1, source_target_pairs={{0,16},{1,17},{2,18},{3,19},{4,0},{5,1},{6,2},{7,3},{8,12},{9,13},... | collective-permute-start | bytes 2359304 | tf_op jit(solution)/shard_map/ppermute | solution.py:192
  20.4 1.2 %normalize.5.refs_5_ = bf16[256,768]{1,0:T(8,128)(2,1)S(1)} custom-call(bf16[1536,768]{1,0:T(8,128)(2,1)} %refs_0_.3), custom_call_target="tpu_custom_call" | custom-call | flops 786432 | bytes 786432 | tf_op jit(solution)/shard_map/normalize/pallas_call | solution.py:76
  21.6 1.9 %collective-permute-start.4 = (bf16[256,768]{1,0:T(8,128)(2,1)S(1)}, bf16[256,768]{1,0:T(8,128)(2,1)S(1)}, u32[]{:S(2)}, u32[]{:S(2)}) collective-permute-start(bf16[256,768]{1,0:T(8,128)(2,1)S(1)} %normalize.5.refs_5_), channel_id=1, source_target_pairs={{0,12},{1,13},{2,14},{3,15},{4,52},{5,53},{6,54},{7,55},{8,56},{9,... | collective-permute-start | bytes 1179656 | tf_op jit(solution)/shard_map/ppermute | solution.py:191
  23.5 0.0 collective-permute-done.refs_6_.refs_4_.refs_5_
  23.5 6.1 %collective-permute-start.5 = (bf16[256,768]{1,0:T(8,128)(2,1)S(1)}, bf16[256,768]{1,0:T(8,128)(2,1)S(1)}, u32[]{:S(2)}, u32[]{:S(2)}) collective-permute-start(bf16[256,768]{1,0:T(8,128)(2,1)S(1)} %normalize.5.refs_5_), channel_id=1, source_target_pairs={{0,16},{1,17},{2,18},{3,19},{4,0},{5,1},{6,2},{7,3},{8,12},{9,13},... | collective-permute-start | bytes 1179656 | tf_op jit(solution)/shard_map/ppermute | solution.py:192
  29.6 0.0 collective-permute-done.1.refs_7_.refs_3_.refs_9_.refs_10_
  29.6 3.2 %products.5 = (f32[12,128]{1,0:T(8,128)S(1)}, f32[12,128]{1,0:T(8,128)S(1)}, f32[12,128]{1,0:T(8,128)S(1)}) custom-call(f32[12,128]{1,0:T(8,128)S(1)} %broadcast_in_dim.3.refs_0_.refs_1_.refs_2_, f32[12,128]{1,0:T(8,128)S(1)} %broadcast_in_dim.3.refs_0_.refs_1_.refs_2_, f32[12,128]{1,0:T(8,128)S(1)} %broadcast_in_dim.3.refs_0_.refs_1_.refs_2_, ...), custom_call_target="tpu_custom_call" | custom-call | flops 2717908992 | bytes 3538944 | tf_op jit(solution)/shard_map/products/pallas_call | solution.py:163
  32.8 0.0 collective-permute-done.2.refs_2_.refs_7_
  32.9 0.9 %products.6 = (f32[12,128]{1,0:T(8,128)S(1)}, f32[12,128]{1,0:T(8,128)S(1)}) custom-call(f32[12,128]{1,0:T(8,128)S(1)} %get-tuple-element.27.refs_0_, f32[12,128]{1,0:T(8,128)S(1)} %get-tuple-element.28.refs_1_, bf16[512,768]{1,0:T(8,128)(2,1)S(1)} %collective-permute-done.2.refs_2_.refs_7_, ...), custom_call_target="tpu_custom_call" | custom-call | flops 603979776 | bytes 786432 | tf_op jit(solution)/shard_map/products/pallas_call | solution.py:163
  33.8 0.6 %collective-permute-done.3.refs_8_.refs_4_ = bf16[512,768]{1,0:T(8,128)(2,1)S(1)} collective-permute-done((bf16[512,768]{1,0:T(8,128)(2,1)S(1)}, bf16[512,768]{1,0:T(8,128)(2,1)S(1)}, u32[]{:S(2)}, u32[]{:S(2)}) %collective-permute-start.3) | collective-permute-done | bytes 786464 | tf_op jit(solution)/shard_map/ppermute | solution.py:192
  34.3 2.5 %products.7 = (f32[12,128]{1,0:T(8,128)S(1)}, f32[12,128]{1,0:T(8,128)S(1)}, f32[12,128]{1,0:T(8,128)S(1)}) custom-call(f32[12,128]{1,0:T(8,128)S(1)} %get-tuple-element.26.refs_0_, f32[12,128]{1,0:T(8,128)S(1)} %get-tuple-element.29.refs_1_, f32[12,128]{1,0:T(8,128)S(1)} %get-tuple-element.30.refs_2_, bf16[784,768]{1,0:T(8,128)(2,1)S(1)} %normalize.3.refs_3_, ...), custom_call_target="tpu_custom_call" | custom-call | flops 2214592512 | bytes 2883584 | tf_op jit(solution)/shard_map/products/pallas_call | solution.py:163
  36.9 0.0 collective-permute-done.4.refs_2_.refs_8_
  36.9 0.8 %products.8 = (f32[12,128]{1,0:T(8,128)S(1)}, f32[12,128]{1,0:T(8,128)S(1)}) custom-call(f32[12,128]{1,0:T(8,128)S(1)} %get-tuple-element.32.refs_0_, f32[12,128]{1,0:T(8,128)S(1)} %get-tuple-element.33.refs_1_, bf16[256,768]{1,0:T(8,128)(2,1)S(1)} %collective-permute-done.4.refs_2_.refs_8_, ...), custom_call_target="tpu_custom_call" | custom-call | flops 503316480 | bytes 655360 | tf_op jit(solution)/shard_map/products/pallas_call | solution.py:163
  37.7 0.9 %collective-permute-done.5.refs_9_ = bf16[256,768]{1,0:T(8,128)(2,1)S(1)} collective-permute-done((bf16[256,768]{1,0:T(8,128)(2,1)S(1)}, bf16[256,768]{1,0:T(8,128)(2,1)S(1)}, u32[]{:S(2)}, u32[]{:S(2)}) %collective-permute-start.5) | collective-permute-done | bytes 393248 | tf_op jit(solution)/shard_map/ppermute | solution.py:192
  38.6 1.6 %products.9 = (f32[12,128]{1,0:T(8,128)S(1)}, f32[12,128]{1,0:T(8,128)S(1)}, f32[12,128]{1,0:T(8,128)S(1)}) custom-call(f32[12,128]{1,0:T(8,128)S(1)} %get-tuple-element.31.refs_0_, f32[12,128]{1,0:T(8,128)S(1)} %get-tuple-element.34.refs_1_, f32[12,128]{1,0:T(8,128)S(1)} %get-tuple-element.35.refs_2_, bf16[784,768]{1,0:T(8,128)(2,1)S(1)} %normalize.3.refs_3_, ...), custom_call_target="tpu_custom_call" | custom-call | flops 1207959552 | bytes 1572864 | tf_op jit(solution)/shard_map/products/pallas_call | solution.py:163
  40.1 2.3 %collective-permute-start.7 = (f32[1536]{0:T(1024)S(1)}, f32[1536]{0:T(1024)S(1)}, u32[]{:S(2)}, u32[]{:S(2)}) collective-permute-start(f32[1536]{0:T(1024)S(1)} %bitcast.8), channel_id=1, source_target_pairs={{0,12},{1,13},{2,14},{3,15},{4,52},{5,53},{6,54},{7,55},{8,56},{9,... | collective-permute-start | bytes 18440 | tf_op jit(solution)/shard_map/ppermute | solution.py:205
  42.4 2.1 %collective-permute-start.6 = (f32[1536]{0:T(1024)S(1)}, f32[1536]{0:T(1024)S(1)}, u32[]{:S(2)}, u32[]{:S(2)}) collective-permute-start(f32[1536]{0:T(1024)S(1)} %bitcast.7), channel_id=1, source_target_pairs={{16,0},{17,1},{18,2},{19,3},{0,4},{1,5},{2,6},{3,7},{12,8},{13,9},... | collective-permute-start | bytes 18440 | tf_op jit(solution)/shard_map/ppermute | solution.py:206
  44.6 2.3 %collective-permute-done.7 = f32[1536]{0:T(1024)S(1)} collective-permute-done((f32[1536]{0:T(1024)S(1)}, f32[1536]{0:T(1024)S(1)}, u32[]{:S(2)}, u32[]{:S(2)}) %collective-permute-start.7) | collective-permute-done | bytes 6176 | tf_op jit(solution)/shard_map/ppermute | solution.py:205
  46.9 4.4 %collective-permute-done.6 = f32[1536]{0:T(1024)S(1)} collective-permute-done((f32[1536]{0:T(1024)S(1)}, f32[1536]{0:T(1024)S(1)}, u32[]{:S(2)}, u32[]{:S(2)}) %collective-permute-start.6) | collective-permute-done | bytes 6176 | tf_op jit(solution)/shard_map/ppermute | solution.py:206
  51.3 0.6 %fusion = f32[1536]{0:T(1024)} fusion(f32[1536]{0:T(1024)S(1)} %collective-permute-done.7, f32[1536]{0:T(1024)S(1)} %collective-permute-done.6, f32[12,128]{1,0:T(8,128)S(1)} %get-tuple-element.36), kind=kLoop, calls=%fused_computation.1 | loop fusion | flops 3072 | bytes 24576 | tf_op jit(solution)/shard_map/max | solution.py:207
  (1 shorter events, 0.0 us)
Async XLA Ops:
  2.2 21.3 %collective-permute-start = (bf16[784,768]{1,0:T(8,128)(2,1)S(1)}, bf16[784,768]{1,0:T(8,128)(2,1)S(1)}, u32[]{:S(2)}, u32[]{:S(2)}) collective-permute-start(bf16[784,768]{1,0:T(8,128)(2,1)S(1)} %normalize.3.refs_3_), channel_id=1, source_target_pairs={{0,12},{1,13},{2,14},{3,15},{4,52},{5,53},{6,54},{7,55},{8,56},{9,... | collective-permute-start | bytes 3612680 | tf_op jit(solution)/shard_map/ppermute | solution.py:185
  7.1 22.5 %collective-permute-start.1 = (bf16[784,768]{1,0:T(8,128)(2,1)S(1)}, bf16[784,768]{1,0:T(8,128)(2,1)S(1)}, u32[]{:S(2)}, u32[]{:S(2)}) collective-permute-start(bf16[784,768]{1,0:T(8,128)(2,1)S(1)} %normalize.3.refs_3_), channel_id=1, source_target_pairs={{0,16},{1,17},{2,18},{3,19},{4,0},{5,1},{6,2},{7,3},{8,12},{9,13},... | collective-permute-start | bytes 3612680 | tf_op jit(solution)/shard_map/ppermute | solution.py:186
  13.3 19.5 %collective-permute-start.2 = (bf16[512,768]{1,0:T(8,128)(2,1)S(1)}, bf16[512,768]{1,0:T(8,128)(2,1)S(1)}, u32[]{:S(2)}, u32[]{:S(2)}) collective-permute-start(bf16[512,768]{1,0:T(8,128)(2,1)S(1)} %normalize.4.refs_4_), channel_id=1, source_target_pairs={{0,12},{1,13},{2,14},{3,15},{4,52},{5,53},{6,54},{7,55},{8,56},{9,... | collective-permute-start | bytes 2359304 | tf_op jit(solution)/shard_map/ppermute | solution.py:191
  15.6 18.7 %collective-permute-start.3 = (bf16[512,768]{1,0:T(8,128)(2,1)S(1)}, bf16[512,768]{1,0:T(8,128)(2,1)S(1)}, u32[]{:S(2)}, u32[]{:S(2)}) collective-permute-start(bf16[512,768]{1,0:T(8,128)(2,1)S(1)} %normalize.4.refs_4_), channel_id=1, source_target_pairs={{0,16},{1,17},{2,18},{3,19},{4,0},{5,1},{6,2},{7,3},{8,12},{9,13},... | collective-permute-start | bytes 2359304 | tf_op jit(solution)/shard_map/ppermute | solution.py:192
  21.6 15.3 %collective-permute-start.4 = (bf16[256,768]{1,0:T(8,128)(2,1)S(1)}, bf16[256,768]{1,0:T(8,128)(2,1)S(1)}, u32[]{:S(2)}, u32[]{:S(2)}) collective-permute-start(bf16[256,768]{1,0:T(8,128)(2,1)S(1)} %normalize.5.refs_5_), channel_id=1, source_target_pairs={{0,12},{1,13},{2,14},{3,15},{4,52},{5,53},{6,54},{7,55},{8,56},{9,... | collective-permute-start | bytes 1179656 | tf_op jit(solution)/shard_map/ppermute | solution.py:191
  23.5 15.1 %collective-permute-start.5 = (bf16[256,768]{1,0:T(8,128)(2,1)S(1)}, bf16[256,768]{1,0:T(8,128)(2,1)S(1)}, u32[]{:S(2)}, u32[]{:S(2)}) collective-permute-start(bf16[256,768]{1,0:T(8,128)(2,1)S(1)} %normalize.5.refs_5_), channel_id=1, source_target_pairs={{0,16},{1,17},{2,18},{3,19},{4,0},{5,1},{6,2},{7,3},{8,12},{9,13},... | collective-permute-start | bytes 1179656 | tf_op jit(solution)/shard_map/ppermute | solution.py:192
  40.1 6.8 %collective-permute-start.7 = (f32[1536]{0:T(1024)S(1)}, f32[1536]{0:T(1024)S(1)}, u32[]{:S(2)}, u32[]{:S(2)}) collective-permute-start(f32[1536]{0:T(1024)S(1)} %bitcast.8), channel_id=1, source_target_pairs={{0,12},{1,13},{2,14},{3,15},{4,52},{5,53},{6,54},{7,55},{8,56},{9,... | collective-permute-start | bytes 18440 | tf_op jit(solution)/shard_map/ppermute | solution.py:205
  42.4 8.9 %collective-permute-start.6 = (f32[1536]{0:T(1024)S(1)}, f32[1536]{0:T(1024)S(1)}, u32[]{:S(2)}, u32[]{:S(2)}) collective-permute-start(f32[1536]{0:T(1024)S(1)} %bitcast.7), channel_id=1, source_target_pairs={{16,0},{17,1},{18,2},{19,3},{0,4},{1,5},{2,6},{3,7},{12,8},{13,9},... | collective-permute-start | bytes 18440 | tf_op jit(solution)/shard_map/ppermute | solution.py:206

commit v5 on v4

v5 whole, which is shorter than its diff:
```python
import functools

import jax
import jax.numpy as jnp
from jax import lax
from jax.experimental import pallas as pl
from jax.experimental.pallas import tpu as pltpu
from jax.sharding import PartitionSpec as P

LANES = 128
TAG_ROWS = 16
CHUNKS = (768, 512, 256)
AXES = ("grp", "pair")


def routes(grp, pair):
    side = 4
    rest = pair // (side * side)
    near, far = [], []
    for g in range(grp):
        for y in range(side):
            for x in range(side):
                for z in range(rest):

                    def at(v, u):
                        return g * pair + (v * side + u) * rest + z

                    owns_y = (y in (1, 2)) ^ (x in (1, 2)) ^ (g % 2 == 1)
                    here = at(y, x)
                    near.append((here, at(y, x ^ 1) if owns_y else at(y ^ 1, x)))
                    far.append((here, at(3 - y, x) if owns_y else at(y, 3 - x)))
    return near, far


def unit_rows(rows):
    wide = rows.astype(jnp.float32)
    squared = jnp.sum(wide * wide, axis=1, keepdims=True)
    return (wide * lax.rsqrt(squared + 1e-06)).astype(jnp.bfloat16)


def head_rows(rows, count, row_counts, ids):
    width = rows.shape[1]

    def kernel(rows_ref, valid_ref, ids_ref, out_ref, held_ids, arrived):
        ids_copy = pltpu.make_async_copy(ids_ref, held_ids, arrived.at[0])
        ids_copy.start()
        copy = pltpu.make_async_copy(rows_ref.at[pl.ds(0, count)], out_ref.at[pl.ds(0, count)], arrived.at[1])
        copy.start()
        ids_copy.wait()
        ids = held_ids[...]
        place = lax.broadcasted_iota(jnp.int32, ids.shape, 0) * LANES
        place = place + lax.broadcasted_iota(jnp.int32, ids.shape, 1)
        tags = jnp.where(place < valid_ref[0], ids, -1).astype(jnp.float32)
        spare = jnp.full((TAG_ROWS - ids.shape[0], LANES), -1.0, jnp.float32)
        out_ref[count:, 0:LANES] = jnp.concatenate([tags, spare], axis=0).astype(jnp.bfloat16)
        out_ref[count:, LANES:] = jnp.zeros((TAG_ROWS, width - LANES), jnp.bfloat16)
        copy.wait()

    in_hbm = pl.BlockSpec(memory_space=pltpu.HBM)
    return pl.pallas_call(
        kernel,
        in_specs=[in_hbm, pl.BlockSpec(memory_space=pltpu.SMEM), in_hbm],
        out_specs=pl.BlockSpec(memory_space=pltpu.VMEM),
        out_shape=pltpu.VMEM((count + TAG_ROWS, width), jnp.bfloat16),
        scratch_shapes=[pltpu.VMEM(ids.shape, jnp.int32), pltpu.SemaphoreType.DMA((2,))],
        cost_estimate=pl.CostEstimate(flops=count, bytes_accessed=4 * count * width, transcendentals=0),
        name="head_rows",
    )(pltpu.with_memory_space_constraint(rows, pltpu.HBM), row_counts, pltpu.with_memory_space_constraint(ids, pltpu.HBM))


def normalize_head(head):
    count, width = head.shape[0] - TAG_ROWS, head.shape[1]

    def kernel(head_ref, out_ref):
        for at in range(0, count, 256):
            out_ref[at : at + 256, :] = unit_rows(head_ref[at : at + 256, :])
        out_ref[count:, :] = head_ref[count:, :]

    whole = pl.BlockSpec(memory_space=pltpu.VMEM)
    return pl.pallas_call(
        kernel,
        in_specs=[whole],
        out_specs=whole,
        out_shape=pltpu.VMEM(head.shape, jnp.bfloat16),
        compiler_params=pltpu.CompilerParams(vmem_limit_bytes=16 << 20),
        cost_estimate=pl.CostEstimate(flops=4 * count * width, bytes_accessed=count * width, transcendentals=count),
        name="normalize_head",
    )(pltpu.with_memory_space_constraint(head, pltpu.VMEM))


def normalize(rows, first, count, step):
    width = rows.shape[1]
    places = [(at, min(step, count - at)) for at in range(0, count, step)]

    def kernel(rows_ref, out_ref, held, arrived):
        copies = [
            pltpu.make_async_copy(rows_ref.at[pl.ds(first + at, size)], held.at[pl.ds(at, size)], arrived.at[i])
            for i, (at, size) in enumerate(places)
        ]
        for copy in copies:
            copy.start()
        for copy, (at, size) in zip(copies, places):
            copy.wait()
            out_ref[at : at + size, :] = unit_rows(held[at : at + size, :])

    return pl.pallas_call(
        kernel,
        in_specs=[pl.BlockSpec(memory_space=pltpu.HBM)],
        out_specs=pl.BlockSpec(memory_space=pltpu.VMEM),
        out_shape=pltpu.VMEM((count, width), jnp.bfloat16),
        scratch_shapes=[pltpu.VMEM((count, width), jnp.bfloat16), pltpu.SemaphoreType.DMA((len(places),))],
        compiler_params=pltpu.CompilerParams(vmem_limit_bytes=16 << 20),
        cost_estimate=pl.CostEstimate(flops=4 * count * width, bytes_accessed=4 * count * width, transcendentals=count),
        name="normalize",
    )(pltpu.with_memory_space_constraint(rows, pltpu.HBM))


def products_kernel(plan, *refs):
    rows, cols, pairs, touched, tag_at, block, n_chunks = plan
    state_in = dict(zip(touched, refs[: len(touched)]))
    refs = refs[len(touched) :]
    chunks = refs[:n_chunks]
    state_out = dict(zip(touched, refs[n_chunks : n_chunks + len(touched)]))
    cacc = refs[-1]

    def tags_of(which):
        ref, at = tag_at[which]
        return chunks[ref][at : at + TAG_ROWS, 0:LANES].astype(jnp.float32)

    row_tags = {which: tags_of(which) for which in {row[0] for row in rows}}
    col_tags = {which: tags_of(which) for which in {col[0] for col in cols}}
    col_tags = {which: jnp.where(tags < 0.0, -2.0, tags) for which, tags in col_tags.items()}
    cacc[...] = jnp.full(cacc.shape, -1.0, jnp.float32)
    for key in touched:
        state_out[key][...] = state_in[key][...]
    for r, (which, ref, start, size) in enumerate(rows):
        mine = [c for c in range(len(cols)) if (r, c) in pairs]
        for i in range(0, size, block):
            height = min(block, size - i)
            left = chunks[ref][i : i + height, :]
            tag = []
            for q in range(0, height, LANES):
                line = row_tags[which][(start + i + q) // LANES][None, :]
                tag.append(jnp.broadcast_to(line, (LANES, LANES)).T)
            tag = jnp.concatenate(tag, axis=0)
            best = jnp.full((height, LANES), -1.0, jnp.float32)
            for c in mine:
                col_which, col_ref, col_start, col_size, base = cols[c]
                for j in range(0, col_size, block):
                    width = min(block, col_size - j)
                    right = chunks[col_ref][j : j + width, :]
                    tile = lax.dot_general(
                        left, right, (((1,), (1,)), ((), ())), preferred_element_type=jnp.float32
                    )
                    for g in range(0, width, LANES):
                        line = col_tags[col_which][(col_start + j + g) // LANES][None, :]
                        part = jnp.where(tag == line, tile[:, g : g + LANES], -1.0)
                        best = jnp.maximum(best, part)
                        at = base + j + g
                        high = jnp.max(part.reshape(height // 8, 8, LANES), axis=0)
                        cacc[:, at : at + LANES] = jnp.maximum(cacc[:, at : at + LANES], high)
            for q in range(0, height, LANES):
                line = jnp.max(best[q : q + LANES, :].T, axis=0, keepdims=True)
                at = (start + i + q) // LANES
                state_out[which][at : at + 1, :] = jnp.maximum(state_out[which][at : at + 1, :], line)
    for which, _, col_start, col_size, base in cols:
        for j in range(0, col_size, LANES):
            line = jnp.max(cacc[:, base + j : base + j + LANES], axis=0, keepdims=True)
            at = (col_start + j) // LANES
            state_out[which][at : at + 1, :] = jnp.maximum(state_out[which][at : at + 1, :], line)


def products(state, want, arrays, sizes, block=512):
    row_keys = sorted({left for left, _ in want})
    col_keys = sorted({right for _, right in want})
    touched = tuple(sorted({w for w, _ in row_keys + col_keys}))
    keys = row_keys + col_keys
    keys += [(w, 0) for w in touched if (w, 0) not in keys]

    def place(key):
        which, chunk = key
        return which, keys.index(key), sum(sizes[which][:chunk]), sizes[which][chunk]

    def width(some):
        return sum(sizes[w][c] for w, c in some)

    rows = tuple(place(key) for key in row_keys)
    cols = tuple(place(key) + (width(col_keys[:i]),) for i, key in enumerate(col_keys))
    pairs = frozenset((row_keys.index(left), col_keys.index(right)) for left, right in want)
    tag_at = {w: (keys.index((w, 0)), sizes[w][0]) for w in touched}
    plan = (rows, cols, pairs, touched, tag_at, block, len(keys))
    operands = [pltpu.with_memory_space_constraint(arrays[w][c], pltpu.VMEM) for w, c in keys]
    before = [state[w] for w in touched]
    depth = operands[0].shape[1]
    whole = pl.BlockSpec(memory_space=pltpu.VMEM)
    macs = sum(width([left]) * width([right]) for left, right in want)
    after = pl.pallas_call(
        functools.partial(products_kernel, plan),
        in_specs=[whole] * (len(before) + len(operands)),
        out_specs=[whole] * len(before),
        out_shape=[jax.ShapeDtypeStruct(s.shape, s.dtype) for s in before],
        scratch_shapes=[pltpu.VMEM((8, width(col_keys)), jnp.float32)],
        compiler_params=pltpu.CompilerParams(vmem_limit_bytes=16 << 20),
        cost_estimate=pl.CostEstimate(flops=2 * macs * depth, bytes_accessed=2 * macs, transcendentals=0),
        name="products",
    )(*before, *operands)
    state = list(state)
    for w, value in zip(touched, after):
        state[w] = value
    return state


def per_device(embeddings, cluster_ids, row_counts, *, near_route, far_route):
    rows = embeddings.shape[0]
    sizes = CHUNKS
    back_route = [(b, a) for a, b in near_route]
    ids = cluster_ids.reshape(rows // LANES, LANES)
    head = head_rows(embeddings, sizes[0], row_counts, ids)
    far = [lax.ppermute(head, AXES, far_route)]
    near = [lax.ppermute(head, AXES, near_route)]
    own = [head]
    start = sizes[0]
    for size in sizes[1:]:
        embeddings, own[-1] = lax.optimization_barrier((embeddings, own[-1]))
        own.append(normalize(embeddings, start, size, 256))
        far.append(lax.ppermute(own[-1], AXES, far_route))
        near.append(lax.ppermute(own[-1], AXES, near_route))
        start += size
    own[0], far[0], near[0] = [normalize_head(h) for h in (own[0], far[0], near[0])]
    state = [jnp.full((rows // LANES, LANES), -1.0, jnp.float32)] * 3
    last = len(sizes) - 1
    every = range(len(sizes))
    fold = functools.partial(products, arrays=(own, far, near), sizes=(sizes,) * 3)
    owns = [(0, r) for r in every]
    fars = [(1, r) for r in every]
    state = fold(state, {(row, (2, 0)) for row in owns + fars[:1]})
    for c in range(1, last):
        state = fold(state, {(fars[c], (2, k)) for k in range(c)})
        state = fold(state, {(row, (2, c)) for row in owns + fars[: c + 1]})
    state = fold(state, {(fars[last], (2, k)) for k in range(last)})
    state = fold(state, {((2, last), col) for col in owns + fars})
    kept, far_best, near_best = [s.reshape(rows) for s in state]
    from_far = lax.ppermute(far_best, AXES, far_route)
    from_near = lax.ppermute(near_best, AXES, back_route)
    return jnp.maximum(jnp.maximum(kept, from_near), from_far)


def solution(mesh):
    near_route, far_route = routes(mesh.shape["grp"], mesh.shape["pair"])
    return jax.shard_map(
        functools.partial(per_device, near_route=near_route, far_route=far_route),
        mesh=mesh,
        in_specs=(P(("grp", "pair"), None), P(("grp", "pair")), P(("grp", "pair"))),
        out_specs=P(("grp", "pair")),
        check_vma=False,
    )
```

time: 52.3 us -> 52 us (level)
  Pallas kernels: 13.1 us -> 13.9 us
  waiting for transfers between devices: 8.17 us -> 7.42 us
    pallas_call x3 -> x6, Pallas kernels: 4.07 us -> 4.91 us  [the longest x2 2.51 us: normalize(): pl.pallas_call(kernel, in_specs=[pl.BlockSpec(memory_space=pltpu.HBM)], o...]
    ppermute x2, waiting for transfers between devices: 1.45 us -> 0.7 us  [per_device(): near.append(lax.ppermute(own[-1], AXES, near_route))]
  transfers between devices with their start and end apart: 8 -> 8, of which waited for: 4 -> 3; matrix products, arithmetic and copies ran while one was open for 0% -> 0% of each run, Pallas kernels for 19% -> 21%
where the time goes in v5:
time: 52 us; the launch traced here: 51.6 us
  starting transfers between devices  28.9 us (56%)
  Pallas kernels  13.9 us (27%)
  waiting for transfers between devices  7.42 us (14%)
  between operations  0.82 us (2%)
  other arithmetic  0.6 us (1%)
    ppermute x2, starting transfers between devices, per_device(): near.append(lax.ppermute(own[-1], AXES, near_route))  10.5 us
    pallas_call x5, Pallas kernels, products(): pl.pallas_call(functools.partial(products_kernel, plan), in_specs=[whole]...  8.99 us
    ppermute x1, starting transfers between devices, per_device(): far = [lax.ppermute(head, AXES, far_route)]  4.92 us
    ppermute x1, starting transfers between devices, per_device(): near = [lax.ppermute(head, AXES, near_route)]  4.81 us
    ppermute x1, waiting for transfers between devices, per_device(): from_near = lax.ppermute(near_best, AXES, back_route)  4.4 us
    ppermute x2, starting transfers between devices, per_device(): far.append(lax.ppermute(own[-1], AXES, far_route))  4.22 us
    pallas_call x2, Pallas kernels, normalize(): pl.pallas_call(kernel, in_specs=[pl.BlockSpec(memory_space=pltpu.HBM)], o...  2.51 us
    ppermute x1, waiting for transfers between devices, per_device(): from_far = lax.ppermute(far_best, AXES, far_route)  2.31 us
  transfers between devices with their start and end apart: 8, of which 3 were waited for; matrix products, arithmetic and copies ran while one was open for 0% of the time, Pallas kernels for 21%

profile of v5, /device:TPU:2, one launch (start us, length us, event | category | flops | bytes accessed | tf_op | source)
XLA Modules:
  0.0 51.6 jit_solution(15727768041426765555)
XLA Ops:
  0.7 1.3 %head_rows.1.head_ref = bf16[784,768]{1,0:T(8,128)(2,1)S(1)} custom-call(bf16[1536,768]{1,0:T(8,128)(2,1)} %rows_ref.3, s32[1]{0:T(128)S(6)} %copy.4.valid_ref, s32[12,128]{1,0:T(8,128)} %bitcast.9), custom_call_target="tpu_custom_call" | custom-call | flops 768 | bytes 2359296 | tf_op jit(solution)/shard_map/head_rows/pallas_call | solution.py:60
  2.0 4.9 %collective-permute-start = (bf16[784,768]{1,0:T(8,128)(2,1)S(1)}, bf16[784,768]{1,0:T(8,128)(2,1)S(1)}, u32[]{:S(2)}, u32[]{:S(2)}) collective-permute-start(bf16[784,768]{1,0:T(8,128)(2,1)S(1)} %head_rows.1.head_ref), channel_id=1, source_target_pairs={{0,12},{1,13},{2,14},{3,15},{4,52},{5,53},{6,54},{7,55},{8,56},{9,... | collective-permute-start | bytes 3612680 | tf_op jit(solution)/shard_map/ppermute | solution.py:219
  6.9 4.8 %collective-permute-start.1 = (bf16[784,768]{1,0:T(8,128)(2,1)S(1)}, bf16[784,768]{1,0:T(8,128)(2,1)S(1)}, u32[]{:S(2)}, u32[]{:S(2)}) collective-permute-start(bf16[784,768]{1,0:T(8,128)(2,1)S(1)} %head_rows.1.head_ref), channel_id=1, source_target_pairs={{0,16},{1,17},{2,18},{3,19},{4,0},{5,1},{6,2},{7,3},{8,12},{9,13},... | collective-permute-start | bytes 3612680 | tf_op jit(solution)/shard_map/ppermute | solution.py:220
  11.7 1.3 %normalize.2.refs_4_.refs_5_ = bf16[512,768]{1,0:T(8,128)(2,1)S(1)} custom-call(bf16[1536,768]{1,0:T(8,128)(2,1)} %rows_ref.3), custom_call_target="tpu_custom_call" | custom-call | flops 1572864 | bytes 1572864 | tf_op jit(solution)/shard_map/normalize/pallas_call | solution.py:106
  13.1 2.3 %collective-permute-start.2 = (bf16[512,768]{1,0:T(8,128)(2,1)S(1)}, bf16[512,768]{1,0:T(8,128)(2,1)S(1)}, u32[]{:S(2)}, u32[]{:S(2)}) collective-permute-start(bf16[512,768]{1,0:T(8,128)(2,1)S(1)} %normalize.2.refs_4_.refs_5_), channel_id=1, source_target_pairs={{0,12},{1,13},{2,14},{3,15},{4,52},{5,53},{6,54},{7,55},{8,56},{9,... | collective-permute-start | bytes 2359304 | tf_op jit(solution)/shard_map/ppermute | solution.py:226
  15.4 4.8 %collective-permute-start.3 = (bf16[512,768]{1,0:T(8,128)(2,1)S(1)}, bf16[512,768]{1,0:T(8,128)(2,1)S(1)}, u32[]{:S(2)}, u32[]{:S(2)}) collective-permute-start(bf16[512,768]{1,0:T(8,128)(2,1)S(1)} %normalize.2.refs_4_.refs_5_), channel_id=1, source_target_pairs={{0,16},{1,17},{2,18},{3,19},{4,0},{5,1},{6,2},{7,3},{8,12},{9,13},... | collective-permute-start | bytes 2359304 | tf_op jit(solution)/shard_map/ppermute | solution.py:227
  20.1 1.2 %normalize.3.refs_5_.refs_6_ = bf16[256,768]{1,0:T(8,128)(2,1)S(1)} custom-call(bf16[1536,768]{1,0:T(8,128)(2,1)} %rows_ref.3), custom_call_target="tpu_custom_call" | custom-call | flops 786432 | bytes 786432 | tf_op jit(solution)/shard_map/normalize/pallas_call | solution.py:106
  21.3 1.9 %collective-permute-start.4 = (bf16[256,768]{1,0:T(8,128)(2,1)S(1)}, bf16[256,768]{1,0:T(8,128)(2,1)S(1)}, u32[]{:S(2)}, u32[]{:S(2)}) collective-permute-start(bf16[256,768]{1,0:T(8,128)(2,1)S(1)} %normalize.3.refs_5_.refs_6_), channel_id=1, source_target_pairs={{0,12},{1,13},{2,14},{3,15},{4,52},{5,53},{6,54},{7,55},{8,56},{9,... | collective-permute-start | bytes 1179656 | tf_op jit(solution)/shard_map/ppermute | solution.py:226
  23.2 0.4 normalize_head.3.refs_3_.refs_4_
  23.6 0.0 collective-permute-done.head_ref
  23.6 5.7 %collective-permute-start.5 = (bf16[256,768]{1,0:T(8,128)(2,1)S(1)}, bf16[256,768]{1,0:T(8,128)(2,1)S(1)}, u32[]{:S(2)}, u32[]{:S(2)}) collective-permute-start(bf16[256,768]{1,0:T(8,128)(2,1)S(1)} %normalize.3.refs_5_.refs_6_), channel_id=1, source_target_pairs={{0,16},{1,17},{2,18},{3,19},{4,0},{5,1},{6,2},{7,3},{8,12},{9,13},... | collective-permute-start | bytes 1179656 | tf_op jit(solution)/shard_map/ppermute | solution.py:227
  29.3 0.4 normalize_head.4.refs_6_.refs_4_.refs_5_.refs_7_
  29.7 0.0 collective-permute-done.1.head_ref
  29.7 0.4 normalize_head.5.refs_7_.refs_3_.refs_9_.refs_10_
  30.1 3.2 %products.5 = (f32[12,128]{1,0:T(8,128)S(1)}, f32[12,128]{1,0:T(8,128)S(1)}, f32[12,128]{1,0:T(8,128)S(1)}) custom-call(f32[12,128]{1,0:T(8,128)S(1)} %broadcast_in_dim.3.refs_0_.refs_1_.refs_2_, f32[12,128]{1,0:T(8,128)S(1)} %broadcast_in_dim.3.refs_0_.refs_1_.refs_2_, f32[12,128]{1,0:T(8,128)S(1)} %broadcast_in_dim.3.refs_0_.refs_1_.refs_2_, ...), custom_call_target="tpu_custom_call" | custom-call | flops 2717908992 | bytes 3538944 | tf_op jit(solution)/shard_map/products/pallas_call | solution.py:197
  33.3 0.0 collective-permute-done.2.refs_2_.refs_7_.refs_8_
  33.3 0.9 %products.6 = (f32[12,128]{1,0:T(8,128)S(1)}, f32[12,128]{1,0:T(8,128)S(1)}) custom-call(f32[12,128]{1,0:T(8,128)S(1)} %get-tuple-element.27.refs_0_, f32[12,128]{1,0:T(8,128)S(1)} %get-tuple-element.28.refs_1_, bf16[512,768]{1,0:T(8,128)(2,1)S(1)} %collective-permute-done.2.refs_2_.refs_7_.refs_8_, ...), custom_call_target="tpu_custom_call" | custom-call | flops 603979776 | bytes 786432 | tf_op jit(solution)/shard_map/products/pallas_call | solution.py:197
  34.2 0.0 collective-permute-done.3.refs_8_.refs_4_
  34.3 2.5 %products.7 = (f32[12,128]{1,0:T(8,128)S(1)}, f32[12,128]{1,0:T(8,128)S(1)}, f32[12,128]{1,0:T(8,128)S(1)}) custom-call(f32[12,128]{1,0:T(8,128)S(1)} %get-tuple-element.26.refs_0_, f32[12,128]{1,0:T(8,128)S(1)} %get-tuple-element.29.refs_1_, f32[12,128]{1,0:T(8,128)S(1)} %get-tuple-element.30.refs_2_, bf16[784,768]{1,0:T(8,128)(2,1)S(1)} %normalize_head.3.refs_3_.refs_4_, ...), custom_call_target="tpu_custom_call" | custom-call | flops 2214592512 | bytes 2883584 | tf_op jit(solution)/shard_map/products/pallas_call | solution.py:197
  36.8 0.0 collective-permute-done.4.refs_2_.refs_9_
  36.8 0.8 %products.8 = (f32[12,128]{1,0:T(8,128)S(1)}, f32[12,128]{1,0:T(8,128)S(1)}) custom-call(f32[12,128]{1,0:T(8,128)S(1)} %get-tuple-element.32.refs_0_, f32[12,128]{1,0:T(8,128)S(1)} %get-tuple-element.33.refs_1_, bf16[256,768]{1,0:T(8,128)(2,1)S(1)} %collective-permute-done.4.refs_2_.refs_9_, ...), custom_call_target="tpu_custom_call" | custom-call | flops 503316480 | bytes 655360 | tf_op jit(solution)/shard_map/products/pallas_call | solution.py:197
  37.6 0.7 %collective-permute-done.5.refs_3_ = bf16[256,768]{1,0:T(8,128)(2,1)S(1)} collective-permute-done((bf16[256,768]{1,0:T(8,128)(2,1)S(1)}, bf16[256,768]{1,0:T(8,128)(2,1)S(1)}, u32[]{:S(2)}, u32[]{:S(2)}) %collective-permute-start.5) | collective-permute-done | bytes 393248 | tf_op jit(solution)/shard_map/ppermute | solution.py:227
  38.3 1.5 %products.9 = (f32[12,128]{1,0:T(8,128)S(1)}, f32[12,128]{1,0:T(8,128)S(1)}, f32[12,128]{1,0:T(8,128)S(1)}) custom-call(f32[12,128]{1,0:T(8,128)S(1)} %get-tuple-element.31.refs_0_, f32[12,128]{1,0:T(8,128)S(1)} %get-tuple-element.34.refs_1_, f32[12,128]{1,0:T(8,128)S(1)} %get-tuple-element.35.refs_2_, bf16[256,768]{1,0:T(8,128)(2,1)S(1)} %collective-permute-done.5.refs_3_, ...), custom_call_target="tpu_custom_call" | custom-call | flops 1207959552 | bytes 1572864 | tf_op jit(solution)/shard_map/products/pallas_call | solution.py:197
  39.8 2.3 %collective-permute-start.7 = (f32[1536]{0:T(1024)S(1)}, f32[1536]{0:T(1024)S(1)}, u32[]{:S(2)}, u32[]{:S(2)}) collective-permute-start(f32[1536]{0:T(1024)S(1)} %bitcast.8), channel_id=1, source_target_pairs={{0,12},{1,13},{2,14},{3,15},{4,52},{5,53},{6,54},{7,55},{8,56},{9,... | collective-permute-start | bytes 18440 | tf_op jit(solution)/shard_map/ppermute | solution.py:243
  42.1 2.1 %collective-permute-start.6 = (f32[1536]{0:T(1024)S(1)}, f32[1536]{0:T(1024)S(1)}, u32[]{:S(2)}, u32[]{:S(2)}) collective-permute-start(f32[1536]{0:T(1024)S(1)} %bitcast.7), channel_id=1, source_target_pairs={{16,0},{17,1},{18,2},{19,3},{0,4},{1,5},{2,6},{3,7},{12,8},{13,9},... | collective-permute-start | bytes 18440 | tf_op jit(solution)/shard_map/ppermute | solution.py:244
  44.3 2.3 %collective-permute-done.7 = f32[1536]{0:T(1024)S(1)} collective-permute-done((f32[1536]{0:T(1024)S(1)}, f32[1536]{0:T(1024)S(1)}, u32[]{:S(2)}, u32[]{:S(2)}) %collective-permute-start.7) | collective-permute-done | bytes 6176 | tf_op jit(solution)/shard_map/ppermute | solution.py:243
  46.6 4.4 %collective-permute-done.6 = f32[1536]{0:T(1024)S(1)} collective-permute-done((f32[1536]{0:T(1024)S(1)}, f32[1536]{0:T(1024)S(1)}, u32[]{:S(2)}, u32[]{:S(2)}) %collective-permute-start.6) | collective-permute-done | bytes 6176 | tf_op jit(solution)/shard_map/ppermute | solution.py:244
  51.0 0.6 %fusion = f32[1536]{0:T(1024)} fusion(f32[1536]{0:T(1024)S(1)} %collective-permute-done.7, f32[1536]{0:T(1024)S(1)} %collective-permute-done.6, f32[12,128]{1,0:T(8,128)S(1)} %get-tuple-element.36), kind=kLoop, calls=%fused_computation.1 | loop fusion | flops 3072 | bytes 24576 | tf_op jit(solution)/shard_map/max | solution.py:245
  (1 shorter events, 0.0 us)
Async XLA Ops:
  2.0 21.6 %collective-permute-start = (bf16[784,768]{1,0:T(8,128)(2,1)S(1)}, bf16[784,768]{1,0:T(8,128)(2,1)S(1)}, u32[]{:S(2)}, u32[]{:S(2)}) collective-permute-start(bf16[784,768]{1,0:T(8,128)(2,1)S(1)} %head_rows.1.head_ref), channel_id=1, source_target_pairs={{0,12},{1,13},{2,14},{3,15},{4,52},{5,53},{6,54},{7,55},{8,56},{9,... | collective-permute-start | bytes 3612680 | tf_op jit(solution)/shard_map/ppermute | solution.py:219
  6.9 22.8 %collective-permute-start.1 = (bf16[784,768]{1,0:T(8,128)(2,1)S(1)}, bf16[784,768]{1,0:T(8,128)(2,1)S(1)}, u32[]{:S(2)}, u32[]{:S(2)}) collective-permute-start(bf16[784,768]{1,0:T(8,128)(2,1)S(1)} %head_rows.1.head_ref), channel_id=1, source_target_pairs={{0,16},{1,17},{2,18},{3,19},{4,0},{5,1},{6,2},{7,3},{8,12},{9,13},... | collective-permute-start | bytes 3612680 | tf_op jit(solution)/shard_map/ppermute | solution.py:220
  13.1 20.3 %collective-permute-start.2 = (bf16[512,768]{1,0:T(8,128)(2,1)S(1)}, bf16[512,768]{1,0:T(8,128)(2,1)S(1)}, u32[]{:S(2)}, u32[]{:S(2)}) collective-permute-start(bf16[512,768]{1,0:T(8,128)(2,1)S(1)} %normalize.2.refs_4_.refs_5_), channel_id=1, source_target_pairs={{0,12},{1,13},{2,14},{3,15},{4,52},{5,53},{6,54},{7,55},{8,56},{9,... | collective-permute-start | bytes 2359304 | tf_op jit(solution)/shard_map/ppermute | solution.py:226
  15.4 18.9 %collective-permute-start.3 = (bf16[512,768]{1,0:T(8,128)(2,1)S(1)}, bf16[512,768]{1,0:T(8,128)(2,1)S(1)}, u32[]{:S(2)}, u32[]{:S(2)}) collective-permute-start(bf16[512,768]{1,0:T(8,128)(2,1)S(1)} %normalize.2.refs_4_.refs_5_), channel_id=1, source_target_pairs={{0,16},{1,17},{2,18},{3,19},{4,0},{5,1},{6,2},{7,3},{8,12},{9,13},... | collective-permute-start | bytes 2359304 | tf_op jit(solution)/shard_map/ppermute | solution.py:227
  21.3 15.5 %collective-permute-start.4 = (bf16[256,768]{1,0:T(8,128)(2,1)S(1)}, bf16[256,768]{1,0:T(8,128)(2,1)S(1)}, u32[]{:S(2)}, u32[]{:S(2)}) collective-permute-start(bf16[256,768]{1,0:T(8,128)(2,1)S(1)} %normalize.3.refs_5_.refs_6_), channel_id=1, source_target_pairs={{0,12},{1,13},{2,14},{3,15},{4,52},{5,53},{6,54},{7,55},{8,56},{9,... | collective-permute-start | bytes 1179656 | tf_op jit(solution)/shard_map/ppermute | solution.py:226
  23.6 14.7 %collective-permute-start.5 = (bf16[256,768]{1,0:T(8,128)(2,1)S(1)}, bf16[256,768]{1,0:T(8,128)(2,1)S(1)}, u32[]{:S(2)}, u32[]{:S(2)}) collective-permute-start(bf16[256,768]{1,0:T(8,128)(2,1)S(1)} %normalize.3.refs_5_.refs_6_), channel_id=1, source_target_pairs={{0,16},{1,17},{2,18},{3,19},{4,0},{5,1},{6,2},{7,3},{8,12},{9,13},... | collective-permute-start | bytes 1179656 | tf_op jit(solution)/shard_map/ppermute | solution.py:227
  39.8 6.8 %collective-permute-start.7 = (f32[1536]{0:T(1024)S(1)}, f32[1536]{0:T(1024)S(1)}, u32[]{:S(2)}, u32[]{:S(2)}) collective-permute-start(f32[1536]{0:T(1024)S(1)} %bitcast.8), channel_id=1, source_target_pairs={{0,12},{1,13},{2,14},{3,15},{4,52},{5,53},{6,54},{7,55},{8,56},{9,... | collective-permute-start | bytes 18440 | tf_op jit(solution)/shard_map/ppermute | solution.py:243
  42.1 8.8 %collective-permute-start.6 = (f32[1536]{0:T(1024)S(1)}, f32[1536]{0:T(1024)S(1)}, u32[]{:S(2)}, u32[]{:S(2)}) collective-permute-start(f32[1536]{0:T(1024)S(1)} %bitcast.7), channel_id=1, source_target_pairs={{16,0},{17,1},{18,2},{19,3},{0,4},{1,5},{2,6},{3,7},{12,8},{13,9},... | collective-permute-start | bytes 18440 | tf_op jit(solution)/shard_map/ppermute | solution.py:244

commit v6 on v5

--- a/solution.py
+++ b/solution.py
@@ -240,9 +240,9 @@
     state = fold(state, {(fars[last], (2, k)) for k in range(last)})
     state = fold(state, {((2, last), col) for col in owns + fars})
     kept, far_best, near_best = [s.reshape(rows) for s in state]
+    from_near = lax.ppermute(near_best, AXES, back_route)
     from_far = lax.ppermute(far_best, AXES, far_route)
-    from_near = lax.ppermute(near_best, AXES, back_route)
-    return jnp.maximum(jnp.maximum(kept, from_near), from_far)
+    return jnp.maximum(kept, jnp.maximum(from_near, from_far))
 
 
 def solution(mesh):

time: 52 us -> 51.9 us (level)
  the two profiles are of different devices: /device:TPU:2 before, /device:TPU:6 now
where the time goes in v6:
time: 51.9 us; the launch traced here: 51.5 us
  starting transfers between devices  24.5 us (47%)
  Pallas kernels  13.9 us (27%)
  waiting for transfers between devices  11.8 us (23%)
  between operations  0.79 us (2%)
  other arithmetic  0.6 us (1%)
    pallas_call x5, Pallas kernels, products(): pl.pallas_call(functools.partial(products_kernel, plan), in_specs=[whole]...  8.98 us
    ppermute x1, starting transfers between devices, per_device(): far = [lax.ppermute(head, AXES, far_route)]  7.76 us
    ppermute x2, starting transfers between devices, per_device(): far.append(lax.ppermute(own[-1], AXES, far_route))  7.05 us
    ppermute x2, waiting for transfers between devices, per_device(): near.append(lax.ppermute(own[-1], AXES, near_route))  3.88 us
    ppermute x2, starting transfers between devices, per_device(): near.append(lax.ppermute(own[-1], AXES, near_route))  3.83 us
    ppermute x1, waiting for transfers between devices, per_device(): from_far = lax.ppermute(far_best, AXES, far_route)  3.14 us
    pallas_call x2, Pallas kernels, normalize(): pl.pallas_call(kernel, in_specs=[pl.BlockSpec(memory_space=pltpu.HBM)], o...  2.51 us
    ppermute x1, starting transfers between devices, per_device(): from_far = lax.ppermute(far_best, AXES, far_route)  2.03 us
  transfers between devices with their start and end apart: 8, of which 7 were waited for; matrix products, arithmetic and copies ran while one was open for 0% of the time, Pallas kernels for 21%

profile of v6, /device:TPU:6, one launch (start us, length us, event | category | flops | bytes accessed | tf_op | source)
XLA Modules:
  0.0 51.5 jit_solution(3081095903493181803)
XLA Ops:
  0.7 1.3 %head_rows.1.head_ref = bf16[784,768]{1,0:T(8,128)(2,1)S(1)} custom-call(bf16[1536,768]{1,0:T(8,128)(2,1)} %rows_ref.3, s32[1]{0:T(128)S(6)} %copy.4.valid_ref, s32[12,128]{1,0:T(8,128)} %bitcast.7), custom_call_target="tpu_custom_call" | custom-call | flops 768 | bytes 2359296 | tf_op jit(solution)/shard_map/head_rows/pallas_call | solution.py:60
  2.0 7.8 %collective-permute-start = (bf16[784,768]{1,0:T(8,128)(2,1)S(1)}, bf16[784,768]{1,0:T(8,128)(2,1)S(1)}, u32[]{:S(2)}, u32[]{:S(2)}) collective-permute-start(bf16[784,768]{1,0:T(8,128)(2,1)S(1)} %head_rows.1.head_ref), channel_id=1, source_target_pairs={{0,12},{1,13},{2,14},{3,15},{4,52},{5,53},{6,54},{7,55},{8,56},{9,... | collective-permute-start | bytes 3612680 | tf_op jit(solution)/shard_map/ppermute | solution.py:219
  9.7 1.9 %collective-permute-start.1 = (bf16[784,768]{1,0:T(8,128)(2,1)S(1)}, bf16[784,768]{1,0:T(8,128)(2,1)S(1)}, u32[]{:S(2)}, u32[]{:S(2)}) collective-permute-start(bf16[784,768]{1,0:T(8,128)(2,1)S(1)} %head_rows.1.head_ref), channel_id=1, source_target_pairs={{0,16},{1,17},{2,18},{3,19},{4,0},{5,1},{6,2},{7,3},{8,12},{9,13},... | collective-permute-start | bytes 3612680 | tf_op jit(solution)/shard_map/ppermute | solution.py:220
  11.7 1.3 %normalize.2.refs_4_.refs_5_ = bf16[512,768]{1,0:T(8,128)(2,1)S(1)} custom-call(bf16[1536,768]{1,0:T(8,128)(2,1)} %rows_ref.3), custom_call_target="tpu_custom_call" | custom-call | flops 1572864 | bytes 1572864 | tf_op jit(solution)/shard_map/normalize/pallas_call | solution.py:106
  13.0 1.9 %collective-permute-start.2 = (bf16[512,768]{1,0:T(8,128)(2,1)S(1)}, bf16[512,768]{1,0:T(8,128)(2,1)S(1)}, u32[]{:S(2)}, u32[]{:S(2)}) collective-permute-start(bf16[512,768]{1,0:T(8,128)(2,1)S(1)} %normalize.2.refs_4_.refs_5_), channel_id=1, source_target_pairs={{0,12},{1,13},{2,14},{3,15},{4,52},{5,53},{6,54},{7,55},{8,56},{9,... | collective-permute-start | bytes 2359304 | tf_op jit(solution)/shard_map/ppermute | solution.py:226
  14.9 1.9 %collective-permute-start.3 = (bf16[512,768]{1,0:T(8,128)(2,1)S(1)}, bf16[512,768]{1,0:T(8,128)(2,1)S(1)}, u32[]{:S(2)}, u32[]{:S(2)}) collective-permute-start(bf16[512,768]{1,0:T(8,128)(2,1)S(1)} %normalize.2.refs_4_.refs_5_), channel_id=1, source_target_pairs={{0,16},{1,17},{2,18},{3,19},{4,0},{5,1},{6,2},{7,3},{8,12},{9,13},... | collective-permute-start | bytes 2359304 | tf_op jit(solution)/shard_map/ppermute | solution.py:227
  16.9 1.2 %normalize.3.refs_5_.refs_6_ = bf16[256,768]{1,0:T(8,128)(2,1)S(1)} custom-call(bf16[1536,768]{1,0:T(8,128)(2,1)} %rows_ref.3), custom_call_target="tpu_custom_call" | custom-call | flops 786432 | bytes 786432 | tf_op jit(solution)/shard_map/normalize/pallas_call | solution.py:106
  18.0 5.1 %collective-permute-start.4 = (bf16[256,768]{1,0:T(8,128)(2,1)S(1)}, bf16[256,768]{1,0:T(8,128)(2,1)S(1)}, u32[]{:S(2)}, u32[]{:S(2)}) collective-permute-start(bf16[256,768]{1,0:T(8,128)(2,1)S(1)} %normalize.3.refs_5_.refs_6_), channel_id=1, source_target_pairs={{0,12},{1,13},{2,14},{3,15},{4,52},{5,53},{6,54},{7,55},{8,56},{9,... | collective-permute-start | bytes 1179656 | tf_op jit(solution)/shard_map/ppermute | solution.py:226
  23.2 0.4 normalize_head.3.refs_3_.refs_4_
  23.6 0.6 %collective-permute-done.head_ref = bf16[784,768]{1,0:T(8,128)(2,1)S(1)} collective-permute-done((bf16[784,768]{1,0:T(8,128)(2,1)S(1)}, bf16[784,768]{1,0:T(8,128)(2,1)S(1)}, u32[]{:S(2)}, u32[]{:S(2)}) %collective-permute-start) | collective-permute-done | bytes 1204256 | tf_op jit(solution)/shard_map/ppermute | solution.py:219
  24.2 1.9 %collective-permute-start.5 = (bf16[256,768]{1,0:T(8,128)(2,1)S(1)}, bf16[256,768]{1,0:T(8,128)(2,1)S(1)}, u32[]{:S(2)}, u32[]{:S(2)}) collective-permute-start(bf16[256,768]{1,0:T(8,128)(2,1)S(1)} %normalize.3.refs_5_.refs_6_), channel_id=1, source_target_pairs={{0,16},{1,17},{2,18},{3,19},{4,0},{5,1},{6,2},{7,3},{8,12},{9,13},... | collective-permute-start | bytes 1179656 | tf_op jit(solution)/shard_map/ppermute | solution.py:227
  26.1 0.4 normalize_head.4.refs_6_.refs_4_.refs_5_.refs_7_
  26.5 1.6 %collective-permute-done.1.head_ref = bf16[784,768]{1,0:T(8,128)(2,1)S(1)} collective-permute-done((bf16[784,768]{1,0:T(8,128)(2,1)S(1)}, bf16[784,768]{1,0:T(8,128)(2,1)S(1)}, u32[]{:S(2)}, u32[]{:S(2)}) %collective-permute-start.1) | collective-permute-done | bytes 1204256 | tf_op jit(solution)/shard_map/ppermute | solution.py:220
  28.1 0.4 normalize_head.5.refs_7_.refs_3_.refs_9_.refs_10_
  28.5 3.2 %products.5 = (f32[12,128]{1,0:T(8,128)S(1)}, f32[12,128]{1,0:T(8,128)S(1)}, f32[12,128]{1,0:T(8,128)S(1)}) custom-call(f32[12,128]{1,0:T(8,128)S(1)} %broadcast_in_dim.3.refs_0_.refs_1_.refs_2_, f32[12,128]{1,0:T(8,128)S(1)} %broadcast_in_dim.3.refs_0_.refs_1_.refs_2_, f32[12,128]{1,0:T(8,128)S(1)} %broadcast_in_dim.3.refs_0_.refs_1_.refs_2_, ...), custom_call_target="tpu_custom_call" | custom-call | flops 2717908992 | bytes 3538944 | tf_op jit(solution)/shard_map/products/pallas_call | solution.py:197
  31.7 0.9 %collective-permute-done.2.refs_2_.refs_7_.refs_8_ = bf16[512,768]{1,0:T(8,128)(2,1)S(1)} collective-permute-done((bf16[512,768]{1,0:T(8,128)(2,1)S(1)}, bf16[512,768]{1,0:T(8,128)(2,1)S(1)}, u32[]{:S(2)}, u32[]{:S(2)}) %collective-permute-start.2) | collective-permute-done | bytes 786464 | tf_op jit(solution)/shard_map/ppermute | solution.py:226
  32.6 0.9 %products.6 = (f32[12,128]{1,0:T(8,128)S(1)}, f32[12,128]{1,0:T(8,128)S(1)}) custom-call(f32[12,128]{1,0:T(8,128)S(1)} %get-tuple-element.27.refs_0_, f32[12,128]{1,0:T(8,128)S(1)} %get-tuple-element.28.refs_1_, bf16[512,768]{1,0:T(8,128)(2,1)S(1)} %collective-permute-done.2.refs_2_.refs_7_.refs_8_, ...), custom_call_target="tpu_custom_call" | custom-call | flops 603979776 | bytes 786432 | tf_op jit(solution)/shard_map/products/pallas_call | solution.py:197
  33.5 3.0 %collective-permute-done.3.refs_8_.refs_4_ = bf16[512,768]{1,0:T(8,128)(2,1)S(1)} collective-permute-done((bf16[512,768]{1,0:T(8,128)(2,1)S(1)}, bf16[512,768]{1,0:T(8,128)(2,1)S(1)}, u32[]{:S(2)}, u32[]{:S(2)}) %collective-permute-start.3) | collective-permute-done | bytes 786464 | tf_op jit(solution)/shard_map/ppermute | solution.py:227
  36.5 2.5 %products.7 = (f32[12,128]{1,0:T(8,128)S(1)}, f32[12,128]{1,0:T(8,128)S(1)}, f32[12,128]{1,0:T(8,128)S(1)}) custom-call(f32[12,128]{1,0:T(8,128)S(1)} %get-tuple-element.26.refs_0_, f32[12,128]{1,0:T(8,128)S(1)} %get-tuple-element.29.refs_1_, f32[12,128]{1,0:T(8,128)S(1)} %get-tuple-element.30.refs_2_, bf16[784,768]{1,0:T(8,128)(2,1)S(1)} %normalize_head.3.refs_3_.refs_4_, ...), custom_call_target="tpu_custom_call" | custom-call | flops 2214592512 | bytes 2883584 | tf_op jit(solution)/shard_map/products/pallas_call | solution.py:197
  39.1 0.0 collective-permute-done.4.refs_2_.refs_9_
  39.1 0.8 %products.8 = (f32[12,128]{1,0:T(8,128)S(1)}, f32[12,128]{1,0:T(8,128)S(1)}) custom-call(f32[12,128]{1,0:T(8,128)S(1)} %get-tuple-element.32.refs_0_, f32[12,128]{1,0:T(8,128)S(1)} %get-tuple-element.33.refs_1_, bf16[256,768]{1,0:T(8,128)(2,1)S(1)} %collective-permute-done.4.refs_2_.refs_9_, ...), custom_call_target="tpu_custom_call" | custom-call | flops 503316480 | bytes 655360 | tf_op jit(solution)/shard_map/products/pallas_call | solution.py:197
  39.9 0.9 %collective-permute-done.5.refs_3_ = bf16[256,768]{1,0:T(8,128)(2,1)S(1)} collective-permute-done((bf16[256,768]{1,0:T(8,128)(2,1)S(1)}, bf16[256,768]{1,0:T(8,128)(2,1)S(1)}, u32[]{:S(2)}, u32[]{:S(2)}) %collective-permute-start.5) | collective-permute-done | bytes 393248 | tf_op jit(solution)/shard_map/ppermute | solution.py:227
  40.7 1.5 %products.9 = (f32[12,128]{1,0:T(8,128)S(1)}, f32[12,128]{1,0:T(8,128)S(1)}, f32[12,128]{1,0:T(8,128)S(1)}) custom-call(f32[12,128]{1,0:T(8,128)S(1)} %get-tuple-element.31.refs_0_, f32[12,128]{1,0:T(8,128)S(1)} %get-tuple-element.34.refs_1_, f32[12,128]{1,0:T(8,128)S(1)} %get-tuple-element.35.refs_2_, bf16[256,768]{1,0:T(8,128)(2,1)S(1)} %collective-permute-done.5.refs_3_, ...), custom_call_target="tpu_custom_call" | custom-call | flops 1207959552 | bytes 1572864 | tf_op jit(solution)/shard_map/products/pallas_call | solution.py:197
  42.3 1.9 %collective-permute-start.6 = (f32[1536]{0:T(1024)S(1)}, f32[1536]{0:T(1024)S(1)}, u32[]{:S(2)}, u32[]{:S(2)}) collective-permute-start(f32[1536]{0:T(1024)S(1)} %bitcast.6), channel_id=1, source_target_pairs={{16,0},{17,1},{18,2},{19,3},{0,4},{1,5},{2,6},{3,7},{12,8},{13,9},... | collective-permute-start | bytes 18440 | tf_op jit(solution)/shard_map/ppermute | solution.py:243
  44.2 2.0 %collective-permute-start.7 = (f32[1536]{0:T(1024)S(1)}, f32[1536]{0:T(1024)S(1)}, u32[]{:S(2)}, u32[]{:S(2)}) collective-permute-start(f32[1536]{0:T(1024)S(1)} %bitcast.5), channel_id=1, source_target_pairs={{0,12},{1,13},{2,14},{3,15},{4,52},{5,53},{6,54},{7,55},{8,56},{9,... | collective-permute-start | bytes 18440 | tf_op jit(solution)/shard_map/ppermute | solution.py:244
  46.2 1.6 %collective-permute-done.6 = f32[1536]{0:T(1024)S(1)} collective-permute-done((f32[1536]{0:T(1024)S(1)}, f32[1536]{0:T(1024)S(1)}, u32[]{:S(2)}, u32[]{:S(2)}) %collective-permute-start.6) | collective-permute-done | bytes 6176 | tf_op jit(solution)/shard_map/ppermute | solution.py:243
  47.8 3.1 %collective-permute-done.7 = f32[1536]{0:T(1024)S(1)} collective-permute-done((f32[1536]{0:T(1024)S(1)}, f32[1536]{0:T(1024)S(1)}, u32[]{:S(2)}, u32[]{:S(2)}) %collective-permute-start.7) | collective-permute-done | bytes 6176 | tf_op jit(solution)/shard_map/ppermute | solution.py:244
  50.9 0.6 %bitcast_maximum_fusion = f32[1536]{0:T(1024)} fusion(f32[12,128]{1,0:T(8,128)S(1)} %get-tuple-element.36, f32[1536]{0:T(1024)S(1)} %collective-permute-done.6, f32[1536]{0:T(1024)S(1)} %collective-permute-done.7), kind=kLoop, calls=%fused_computation | loop fusion | flops 3072 | bytes 24576 | tf_op jit(solution)/shard_map/max | solution.py:245
  (1 shorter events, 0.0 us)
Async XLA Ops:
  2.0 22.2 %collective-permute-start = (bf16[784,768]{1,0:T(8,128)(2,1)S(1)}, bf16[784,768]{1,0:T(8,128)(2,1)S(1)}, u32[]{:S(2)}, u32[]{:S(2)}) collective-permute-start(bf16[784,768]{1,0:T(8,128)(2,1)S(1)} %head_rows.1.head_ref), channel_id=1, source_target_pairs={{0,12},{1,13},{2,14},{3,15},{4,52},{5,53},{6,54},{7,55},{8,56},{9,... | collective-permute-start | bytes 3612680 | tf_op jit(solution)/shard_map/ppermute | solution.py:219
  9.7 18.4 %collective-permute-start.1 = (bf16[784,768]{1,0:T(8,128)(2,1)S(1)}, bf16[784,768]{1,0:T(8,128)(2,1)S(1)}, u32[]{:S(2)}, u32[]{:S(2)}) collective-permute-start(bf16[784,768]{1,0:T(8,128)(2,1)S(1)} %head_rows.1.head_ref), channel_id=1, source_target_pairs={{0,16},{1,17},{2,18},{3,19},{4,0},{5,1},{6,2},{7,3},{8,12},{9,13},... | collective-permute-start | bytes 3612680 | tf_op jit(solution)/shard_map/ppermute | solution.py:220
  13.0 19.6 %collective-permute-start.2 = (bf16[512,768]{1,0:T(8,128)(2,1)S(1)}, bf16[512,768]{1,0:T(8,128)(2,1)S(1)}, u32[]{:S(2)}, u32[]{:S(2)}) collective-permute-start(bf16[512,768]{1,0:T(8,128)(2,1)S(1)} %normalize.2.refs_4_.refs_5_), channel_id=1, source_target_pairs={{0,12},{1,13},{2,14},{3,15},{4,52},{5,53},{6,54},{7,55},{8,56},{9,... | collective-permute-start | bytes 2359304 | tf_op jit(solution)/shard_map/ppermute | solution.py:226
  14.9 21.6 %collective-permute-start.3 = (bf16[512,768]{1,0:T(8,128)(2,1)S(1)}, bf16[512,768]{1,0:T(8,128)(2,1)S(1)}, u32[]{:S(2)}, u32[]{:S(2)}) collective-permute-start(bf16[512,768]{1,0:T(8,128)(2,1)S(1)} %normalize.2.refs_4_.refs_5_), channel_id=1, source_target_pairs={{0,16},{1,17},{2,18},{3,19},{4,0},{5,1},{6,2},{7,3},{8,12},{9,13},... | collective-permute-start | bytes 2359304 | tf_op jit(solution)/shard_map/ppermute | solution.py:227
  18.0 21.0 %collective-permute-start.4 = (bf16[256,768]{1,0:T(8,128)(2,1)S(1)}, bf16[256,768]{1,0:T(8,128)(2,1)S(1)}, u32[]{:S(2)}, u32[]{:S(2)}) collective-permute-start(bf16[256,768]{1,0:T(8,128)(2,1)S(1)} %normalize.3.refs_5_.refs_6_), channel_id=1, source_target_pairs={{0,12},{1,13},{2,14},{3,15},{4,52},{5,53},{6,54},{7,55},{8,56},{9,... | collective-permute-start | bytes 1179656 | tf_op jit(solution)/shard_map/ppermute | solution.py:226
  24.2 16.6 %collective-permute-start.5 = (bf16[256,768]{1,0:T(8,128)(2,1)S(1)}, bf16[256,768]{1,0:T(8,128)(2,1)S(1)}, u32[]{:S(2)}, u32[]{:S(2)}) collective-permute-start(bf16[256,768]{1,0:T(8,128)(2,1)S(1)} %normalize.3.refs_5_.refs_6_), channel_id=1, source_target_pairs={{0,16},{1,17},{2,18},{3,19},{4,0},{5,1},{6,2},{7,3},{8,12},{9,13},... | collective-permute-start | bytes 1179656 | tf_op jit(solution)/shard_map/ppermute | solution.py:227
  42.3 5.5 %collective-permute-start.6 = (f32[1536]{0:T(1024)S(1)}, f32[1536]{0:T(1024)S(1)}, u32[]{:S(2)}, u32[]{:S(2)}) collective-permute-start(f32[1536]{0:T(1024)S(1)} %bitcast.6), channel_id=1, source_target_pairs={{16,0},{17,1},{18,2},{19,3},{0,4},{1,5},{2,6},{3,7},{12,8},{13,9},... | collective-permute-start | bytes 18440 | tf_op jit(solution)/shard_map/ppermute | solution.py:243
  44.2 6.8 %collective-permute-start.7 = (f32[1536]{0:T(1024)S(1)}, f32[1536]{0:T(1024)S(1)}, u32[]{:S(2)}, u32[]{:S(2)}) collective-permute-start(f32[1536]{0:T(1024)S(1)} %bitcast.5), channel_id=1, source_target_pairs={{0,12},{1,13},{2,14},{3,15},{4,52},{5,53},{6,54},{7,55},{8,56},{9,... | collective-permute-start | bytes 18440 | tf_op jit(solution)/shard_map/ppermute | solution.py:244
